TPU v7x, 32 devices: a whole 2x2x4 slice. The times are simulated.
32 devices in a mesh: groups: 2 (over y), exp: 16 (over z, x, core), base: 1.
Axes of the slice: x: 2, y: 2, z: 4, core: 2. Of those that a mesh axis runs over, the one named last changes fastest.
Arguments:
- tokens: bfloat16 [512, 7168], P(('groups', 'exp', 'base')), parts along dimension 0, may hold values from -6 to 6
- routes: int32 [512, 8], P(('groups', 'exp', 'base')), parts along dimension 0, may hold values from 0 to 15, all different within a row; in each aligned block of 16 rows (0 to 15, 16 to 31, ...) at most 12 rows name the same one
- route_weight: float32 [512, 8], P(('groups', 'exp', 'base')), parts along dimension 0, may hold values from 0.03 to 0.6
- base_index: int32 [16, 8], replicated, may hold values from 0 to 55, as said below
- expert_mask: int32 [16, 16, 8], P('exp'), may hold values 0 or 1
- base_gate: bfloat16 [16, 8, 128, 128], P('base'), may hold values from -0.1875 to 0.1875
- base_up: bfloat16 [16, 8, 128, 128], P('base'), may hold values from -0.1875 to 0.1875
- base_down: bfloat16 [16, 8, 128, 128], P('base'), may hold values from -0.375 to 0.375
- delta_in: bfloat16 [16, 7168, 128], P('exp'), may hold values from -0.0625 to 0.0625
- delta_gate_up: bfloat16 [16, 2, 128, 2048], P('exp', None, None, 'base'), may hold values from -0.5 to 0.5
- delta_down_in: bfloat16 [16, 2048, 128], P('exp', 'base'), may hold values from -0.125 to 0.125
- delta_out: bfloat16 [16, 128, 7168], P('exp'), may hold values from -0.5 to 0.5
Outputs:
- combined: bfloat16 [512, 7168], P(('groups', 'exp', 'base')), parts along dimension 0
There are 2 independent parts, one for each index of `groups`. A program takes and returns all parts, laid end to end along the dimension named above; an argument that names none is the same for every part. Nothing has to cross between parts.
Inputs may be any that keep to these rules, and one draw needn't show every extreme that they name: `routes`: in the rows of one device (aligned blocks of 16 tokens) no expert is named by more than 12 tokens, and the 8 experts of a token differ. `base_index`: the 8 entries of each row differ.
All inputs are finite; a program needn't handle non-finite values. No bound on the sum of `expert_mask` on one device may be relied on, other than what follows from the above.
Results may differ from a plain program's by a relative error of at most 0.0071.
Values may be sent and summed in bfloat16 or wider, within the bound.
A program may use at most 128 MiB of HBM per device.

v0:
```python
import jax
import jax.numpy as jnp
from jax import lax
from jax.sharding import PartitionSpec as P


def place_rows(route_block, experts, most_rows, copies, copy_index):
    flat_routes = route_block.reshape(-1)
    onehot = (flat_routes[:, None] == jnp.arange(experts, dtype=jnp.int32)[None, :]).astype(
        jnp.int32
    )
    before = jnp.cumsum(onehot, axis=0) - onehot
    slot_index = jnp.sum(before * onehot, axis=1)
    return (flat_routes * copies + copy_index) * most_rows + slot_index


def spread_matrix(targets, slot_count, choose):
    matches = targets[None, :] == jnp.arange(slot_count, dtype=jnp.int32)[:, None]
    return jnp.any(matches.reshape(slot_count, -1, choose), axis=2).astype(jnp.bfloat16)


def hidden_units(incoming, index_part, keep_part, gate_tiles, up_tiles, delta_first, lift):
    row_count, model_width = incoming.shape
    blocks = model_width // 128
    count_blocks, per_block = index_part.shape
    picked = jnp.take(incoming.reshape(row_count, blocks, 128), index_part.reshape(-1), axis=1)
    picked = picked.reshape(row_count, count_blocks, per_block, 128)
    tile_keep = keep_part.astype(jnp.bfloat16)[:, :, None, None]
    pre_gate = jnp.einsum(
        "rfkc,fkch->rfh", picked, gate_tiles * tile_keep, preferred_element_type=jnp.float32
    ).reshape(row_count, -1)
    pre_up = jnp.einsum(
        "rfkc,fkch->rfh", picked, up_tiles * tile_keep, preferred_element_type=jnp.float32
    ).reshape(row_count, -1)
    lowrank = jnp.dot(incoming, delta_first, preferred_element_type=jnp.float32).astype(
        jnp.bfloat16
    )
    lifted = jnp.einsum("rq,gqh->grh", lowrank, lift, preferred_element_type=jnp.float32)
    return (jax.nn.silu(pre_gate + lifted[0]) * (pre_up + lifted[1])).astype(jnp.bfloat16)


def share_partial(hidden_part, index_part, keep_part, down_tiles, squeeze, delta_last):
    row_count = hidden_part.shape[0]
    count_blocks = down_tiles.shape[0]
    model_width = delta_last.shape[1]
    tile_keep = keep_part.astype(jnp.bfloat16)[:, :, None, None]
    pieces = jnp.einsum(
        "rfh,fkhc->rfkc",
        hidden_part.reshape(row_count, count_blocks, 128),
        down_tiles * tile_keep,
        preferred_element_type=jnp.float32,
    )
    placed = (
        jnp.zeros((row_count, model_width // 128, 128), jnp.float32)
        .at[:, index_part.reshape(-1)]
        .add(pieces.reshape(row_count, -1, 128))
    )
    squeezed = jnp.dot(hidden_part, squeeze, preferred_element_type=jnp.float32).astype(
        jnp.bfloat16
    )
    return placed.reshape(row_count, model_width) + jnp.dot(
        squeezed, delta_last, preferred_element_type=jnp.float32
    )


def per_device(
    tokens,
    routes,
    route_weight,
    base_index,
    expert_mask,
    base_gate,
    base_up,
    base_down,
    delta_in,
    delta_gate_up,
    delta_down_in,
    delta_out,
):
    tok_count, model_width = tokens.shape
    choose = routes.shape[1]
    exp_size = lax.axis_size("exp")
    base_size = lax.axis_size("base")
    half_blocks = base_gate.shape[0]
    most_rows = min(tok_count, max(2, (tok_count * choose + exp_size - 1) // exp_size * 3 // 2))
    own_targets = place_rows(routes, exp_size, most_rows, 1, 0)
    offset = lax.axis_index("base") * half_blocks
    my_index = lax.dynamic_slice_in_dim(base_index, offset, half_blocks, 0)
    my_keep = lax.dynamic_slice_in_dim(expert_mask[0], offset, half_blocks, 0)
    pair_tokens, pair_routes = (
        lax.all_gather(tokens, "base", axis=0, tiled=True),
        lax.all_gather(routes.astype(jnp.bfloat16), "base", axis=0, tiled=True),
    )
    pair_routes = pair_routes.astype(jnp.int32)
    targets = jnp.concatenate(
        [
            place_rows(
                pair_routes[copy_index * tok_count : (copy_index + 1) * tok_count],
                exp_size,
                most_rows,
                base_size,
                copy_index,
            )
            for copy_index in range(base_size)
        ]
    )
    spread = spread_matrix(targets, exp_size * base_size * most_rows, choose)
    outgoing = jnp.dot(spread, pair_tokens, preferred_element_type=jnp.float32).astype(jnp.bfloat16)
    outgoing = outgoing.reshape(exp_size, base_size * most_rows, model_width)
    arrived = lax.all_to_all(outgoing, "exp", split_axis=0, concat_axis=0, tiled=True)
    incoming = arrived.reshape(-1, model_width)
    hidden = hidden_units(
        incoming, my_index, my_keep, base_gate, base_up, delta_in[0], delta_gate_up[0]
    )
    partial_value = share_partial(
        hidden, my_index, my_keep, base_down, delta_down_in[0], delta_out[0]
    )
    summed = lax.psum_scatter(
        partial_value.reshape(exp_size, base_size, most_rows, model_width).astype(jnp.bfloat16),
        "base",
        scatter_dimension=1,
        tiled=True,
    )
    results = summed.reshape(exp_size, most_rows, model_width)
    returned = lax.all_to_all(results, "exp", split_axis=0, concat_axis=0, tiled=True).reshape(
        exp_size * most_rows, model_width
    )
    gathered = returned[own_targets.reshape(tok_count, choose)]
    combined = jnp.sum(route_weight[:, :, None] * gathered.astype(jnp.float32), axis=1)
    return combined.astype(jnp.bfloat16)


def solution(mesh):
    return jax.shard_map(
        per_device,
        mesh=mesh,
        in_specs=(
            P(("groups", "exp", "base"), None),
            P(("groups", "exp", "base"), None),
            P(("groups", "exp", "base"), None),
            P(),
            P("exp", None, None),
            P("base", None, None, None),
            P("base", None, None, None),
            P("base", None, None, None),
            P("exp", None, None),
            P("exp", None, None, "base"),
            P("exp", "base", None),
            P("exp", None, None),
        ),
        out_specs=P(("groups", "exp", "base"), None),
        check_vma=False,
    )
```

profile of v0, /device:TPU:16, one launch (start us, length us, event | category | flops | bytes accessed | tf_op | source)
XLA Modules:
  0.0 294.3 jit_solution(10770014938961716735)
XLA Ops:
  0.0 0.9 copy.43
  1.1 0.1 fusion.38
  1.2 0.2 reduce_window_sum.17
  1.4 0.2 select_reduce_fusion.1
  1.6 0.1 fusion.37
  1.7 0.2 reduce_window_sum.18
  1.9 0.2 select_reduce_fusion
  2.2 0.1 fusion.36
  2.3 3.4 %convolution_convert_fusion = bf16[192,7168]{1,0:T(8,128)(2,1)} fusion(pred[192,16]{0,1:T(8,128)(4,1)S(1)} %fusion.36, bf16[16,7168]{1,0:T(8,128)(2,1)} %param.12), kind=kOutput, calls=%fused_computation.5 | convolution fusion | flops 45416448 | bytes 2984960 | tf_op jit(solution)/shard_map/dot_general | solution.py:108
  5.7 4.5 %reshape.102 = bf16[16,12,7168]{2,1,0:T(8,128)(2,1)} reshape(bf16[192,7168]{1,0:T(8,128)(2,1)} %convolution_convert_fusion) | data formatting | bytes 5505024 | tf_op jit(solution)/shard_map/reshape | solution.py:109
  10.2 6.3 %all-to-all-start = ((bf16[16,12,7168]{2,1,0:T(8,128)(2,1)}), bf16[16,12,7168]{2,1,0:T(8,128)(2,1)}, u32[]{:S(2)}, u32[]{:S(2)}) async-start(bf16[16,12,7168]{2,1,0:T(8,128)(2,1)} %reshape.102), calls=%async_computation | async-start | bytes 7340032 | tf_op jit(solution)/shard_map/all_to_all | solution.py:110
  16.8 81.2 %all-to-all-done = bf16[16,12,7168]{2,1,0:T(8,128)(2,1)} async-done(((bf16[16,12,7168]{2,1,0:T(8,128)(2,1)}), bf16[16,12,7168]{2,1,0:T(8,128)(2,1)}, u32[]{:S(2)}, u32[]{:S(2)}) %all-to-all-start) | async-done | bytes 2752544 | tf_op jit(solution)/shard_map/all_to_all | solution.py:110
  97.9 5.9 %reshape_reshape.3 = bf16[192,56,128]{2,1,0:T(8,128)(2,1)} reshape(bf16[16,12,7168]{2,1,0:T(8,128)(2,1)} %all-to-all-done) | data formatting | bytes 5505024 | tf_op jit(solution)/shard_map/reshape;reshape | solution.py:26
  103.8 4.1 %copy.44 = bf16[192,56,128]{2,0,1:T(8,128)(2,1)} copy(bf16[192,56,128]{2,1,0:T(8,128)(2,1)} %reshape_reshape.3) | data formatting | bytes 5505024 | tf_op jit(solution)/shard_map/reshape;reshape | solution.py:26
  107.9 4.6 %reshape.103 = bf16[192,7168]{1,0:T(8,128)(2,1)} reshape(bf16[16,12,7168]{2,1,0:T(8,128)(2,1)} %all-to-all-done) | data formatting | bytes 5505024 | tf_op jit(solution)/shard_map/reshape | solution.py:111
  112.5 5.4 %convolution_bitcast_fusion = f32[2,192,2048]{2,1,0:T(8,128)} fusion(bf16[1,2,128,2048]{3,2,1,0:T(8,128)(2,1)S(1)} %copy-done.5, bf16[192,7168]{1,0:T(8,128)(2,1)} %reshape.103, bf16[1,7168,128]{2,1,0:T(8,128)(2,1)} %param.20), kind=kOutput, calls=%fused_computation.17 | convolution fusion | flops 553672704 | bytes 8781824 | tf_op jit(solution)/shard_map/rq,gqh->grh/dot_general | solution.py:38
  117.8 2.1 slice_bitcast_fusion.1
  119.9 1.4 copy.56
  121.4 1.4 copy.57
  122.8 5.8 %gather_fusion = bf16[128,192,128]{2,1,0:T(8,128)(2,1)} fusion(bf16[192,56,128]{2,0,1:T(8,128)(2,1)} %copy.44, s32[1024]{0:T(1024)S(1)} %pad_clamp_fusion.1), kind=kCustom, calls=%fused_computation | custom fusion | bytes 12583424 | tf_op jit(solution)/shard_map/jit(_take)/gather | solution.py:26
  128.6 6.7 %fusion.1 = f32[16,128,192,1]{1,2,3,0:T(8,128)S(1)} fusion(bf16[192,16,8,128]{3,0,2,1:T(8,128)(2,1)} %bitcast.87, pred[16,8]{1,0:T(8,128)(4,1)S(1)} %compare_and_fusion, bf16[16,8,128,128]{3,2,1,0:T(8,128)(2,1)} %param.17, bf16[16,8]{1,0:T(8,128)(2,1)S(1)} %copy.39), kind=kOutput, calls=%fused_computation.7 | convolution fusion | flops 816840704 | bytes 12059008 | tf_op jit(solution)/shard_map/rfkc,fkch->rfh/dot_general | solution.py:29
  135.3 6.0 %fusion.17 = bf16[192,16,128]{2,0,1:T(8,128)(2,1)S(1)} fusion(f32[192,16,128]{2,1,0:T(8,128)S(1)} %bitcast.90, f32[192,16,128]{2,1,0:T(8,128)S(1)} %bitcast.89, f32[16,128,192,1]{1,2,3,0:T(8,128)S(1)} %fusion.1, bf16[16,8,128,128]{3,2,1,0:T(8,128)(2,1)} %param.18, bf16[16,8]{1,0:T(8,128)(2,1)S(1)} %copy.39, bf16[192,16,8,128]{3,0,2,1:T(8,128)(2,1)S(1)} %bitcast.88, ...), kind=kOutput, calls=%fused_computation.28 | convolution fusion | flops 819986432 | bytes 15991168 | tf_op jit(solution)/shard_map/rfkc,fkch->rfh/dot_general | solution.py:32
  141.4 6.4 %fusion.5 = f32[16,8,128,192]{2,3,1,0:T(8,128)} fusion(bf16[16,8,128,128]{3,2,1,0:T(8,128)(2,1)S(1)} %copy-done.2, bf16[16,8]{1,0:T(8,128)(2,1)S(1)} %copy.39, bf16[192,16,128]{2,0,1:T(8,128)(2,1)S(1)} %fusion.17), kind=kOutput, calls=%fused_computation.11 | convolution fusion | flops 813694976 | bytes 17563904 | tf_op jit(solution)/shard_map/rfh,fkhc->rfkc/dot_general | solution.py:47
  147.8 3.0 %broadcast_in_dim.14 = f32[192,56,128]{2,0,1:T(8,128)} broadcast(f32[]{:T(128)} %constant.14.clone.1), dimensions={} | broadcast | bytes 5505028 | tf_op jit(solution)/shard_map/broadcast_in_dim | solution.py:54
  150.8 32.7 %scatter_fusion = f32[192,56,128]{2,0,1:T(8,128)} fusion(f32[192,56,128]{2,0,1:T(8,128)} %broadcast_in_dim.14, s32[128]{0:T(128)S(1)} %fusion.39, f32[128,192,128]{2,1,0:T(8,128)} %bitcast.86), kind=kCustom, calls=%fused_computation.2 | custom fusion | flops 3145728 | bytes 37749248 | tf_op jit(solution)/shard_map/scatter-add | solution.py:56
  183.6 5.3 %fusion = bf16[192,7168]{1,0:T(8,128)(2,1)} fusion(bf16[1,128,7168]{2,1,0:T(8,128)(2,1)S(1)} %copy-done, bf16[1,2048,128]{2,1,0:T(8,128)(2,1)S(1)} %copy-done.6, f32[192,56,128]{2,0,1:T(8,128)} %scatter_fusion, bf16[192,16,128]{2,0,1:T(8,128)(2,1)S(1)} %fusion.17), kind=kOutput, calls=%fused_computation.4 | convolution fusion | flops 455761920 | bytes 11403264 | tf_op jit(solution)/shard_map/dot_general | solution.py:61
  188.9 4.5 %convert_element_type.66 = bf16[16,12,7168]{2,1,0:T(8,128)(2,1)} reshape(bf16[192,7168]{1,0:T(8,128)(2,1)} %fusion) | data formatting | bytes 5505024 | tf_op jit(solution)/shard_map/convert_element_type | solution.py:119
  193.3 4.8 %all-to-all-start.1 = ((bf16[16,12,7168]{2,1,0:T(8,128)(2,1)}), bf16[16,12,7168]{2,1,0:T(8,128)(2,1)}, u32[]{:S(2)}, u32[]{:S(2)}) async-start(bf16[16,12,7168]{2,1,0:T(8,128)(2,1)} %convert_element_type.66), calls=%async_computation.1 | async-start | bytes 7340032 | tf_op jit(solution)/shard_map/all_to_all | solution.py:125
  198.3 81.3 %all-to-all-done.1 = bf16[16,12,7168]{2,1,0:T(8,128)(2,1)} async-done(((bf16[16,12,7168]{2,1,0:T(8,128)(2,1)}), bf16[16,12,7168]{2,1,0:T(8,128)(2,1)}, u32[]{:S(2)}, u32[]{:S(2)}) %all-to-all-start.1) | async-done | bytes 2752544 | tf_op jit(solution)/shard_map/all_to_all | solution.py:125
  279.6 4.5 %reshape.106 = bf16[192,7168]{1,0:T(8,128)(2,1)} reshape(bf16[16,12,7168]{2,1,0:T(8,128)(2,1)} %all-to-all-done.1) | data formatting | bytes 5505024 | tf_op jit(solution)/shard_map/reshape | solution.py:125
  284.0 6.8 %gather_fusion.1 = bf16[128,7168]{1,0:T(8,128)(2,1)} fusion(bf16[192,7168]{1,0:T(8,128)(2,1)} %reshape.106, s32[1024]{0:T(1024)S(1)} %pad_clamp_fusion), kind=kCustom, calls=%fused_computation.1 | custom fusion | bytes 3670528 | tf_op jit(solution)/shard_map/gather | solution.py:128
  290.8 3.5 %fusion.7 = bf16[16,7168]{1,0:T(8,128)(2,1)} fusion(bf16[128,7168]{1,0:T(8,128)(2,1)} %gather_fusion.1, f32[16,8]{1,0:T(8,128)S(1)} %copy.37), kind=kLoop, calls=%fused_computation.14 | loop fusion | flops 2637824 | bytes 2064896 | tf_op jit(solution)/shard_map/reduce_sum | solution.py:129
  (36 shorter events, 0.8 us)
Async XLA Ops:
  0.0 183.6 %copy-start = (bf16[1,128,7168]{2,1,0:T(8,128)(2,1)S(1)}, bf16[1,128,7168]{2,1,0:T(8,128)(2,1)}, u32[]{:S(2)}) copy-start(bf16[1,128,7168]{2,1,0:T(8,128)(2,1)} %param.23) | copy-start | bytes 5505028
  10.2 6.3 %copy-start.7 = (s32[16,8]{0,1:T(8,128)S(1)}, s32[16,8]{0,1:T(8,128)}, u32[]{:S(2)}) copy-start(s32[16,8]{0,1:T(8,128)} %param.15) | copy-start | bytes 1540
  10.2 6.5 %copy-start.9 = (s32[1,16,8]{1,2,0:T(8,128)S(1)}, s32[1,16,8]{1,2,0:T(8,128)}, u32[]{:S(2)}) copy-start(s32[1,16,8]{1,2,0:T(8,128)} %param.16) | copy-start | bytes 1540
  10.2 87.7 %all-to-all-start = ((bf16[16,12,7168]{2,1,0:T(8,128)(2,1)}), bf16[16,12,7168]{2,1,0:T(8,128)(2,1)}, u32[]{:S(2)}, u32[]{:S(2)}) async-start(bf16[16,12,7168]{2,1,0:T(8,128)(2,1)} %reshape.102), calls=%async_computation | async-start | bytes 7340032 | tf_op jit(solution)/shard_map/all_to_all | solution.py:110
  107.9 4.6 %copy-start.5 = (bf16[1,2,128,2048]{3,2,1,0:T(8,128)(2,1)S(1)}, bf16[1,2,128,2048]{3,2,1,0:T(8,128)(2,1)}, u32[]{:S(2)}) copy-start(bf16[1,2,128,2048]{3,2,1,0:T(8,128)(2,1)} %param.21) | copy-start | bytes 3145732
  128.6 6.7 %copy-start.1 = (bf16[128,192,128]{2,1,0:T(8,128)(2,1)S(1)}, bf16[128,192,128]{2,1,0:T(8,128)(2,1)}, u32[]{:S(2)}) copy-start(bf16[128,192,128]{2,1,0:T(8,128)(2,1)} %gather_fusion) | copy-start | bytes 18874372
  128.6 6.7 %copy-start.3 = (f32[24,8,16,128]{3,2,1,0:T(8,128)S(1)}, f32[24,8,16,128]{3,2,1,0:T(8,128)}, u32[]{:S(2)}) copy-start(f32[24,8,16,128]{3,2,1,0:T(8,128)} %copy.56) | copy-start | bytes 4718596
  128.6 6.7 %copy-start.4 = (f32[24,8,16,128]{3,2,1,0:T(8,128)S(1)}, f32[24,8,16,128]{3,2,1,0:T(8,128)}, u32[]{:S(2)}) copy-start(f32[24,8,16,128]{3,2,1,0:T(8,128)} %copy.57) | copy-start | bytes 4718596
  135.3 6.0 %copy-start.2 = (bf16[16,8,128,128]{3,2,1,0:T(8,128)(2,1)S(1)}, bf16[16,8,128,128]{3,2,1,0:T(8,128)(2,1)}, u32[]{:S(2)}) copy-start(bf16[16,8,128,128]{3,2,1,0:T(8,128)(2,1)} %param.19) | copy-start | bytes 12582916
  150.8 32.7 %copy-start.6 = (bf16[1,2048,128]{2,1,0:T(8,128)(2,1)S(1)}, bf16[1,2048,128]{2,1,0:T(8,128)(2,1)}, u32[]{:S(2)}) copy-start(bf16[1,2048,128]{2,1,0:T(8,128)(2,1)} %param.22) | copy-start | bytes 1572868
  193.3 4.9 %copy-start.8 = (f32[16,8]{0,1:T(8,128)S(1)}, f32[16,8]{0,1:T(8,128)}, u32[]{:S(2)}) copy-start(f32[16,8]{0,1:T(8,128)} %param.14) | copy-start | bytes 1540
  193.3 86.3 %all-to-all-start.1 = ((bf16[16,12,7168]{2,1,0:T(8,128)(2,1)}), bf16[16,12,7168]{2,1,0:T(8,128)(2,1)}, u32[]{:S(2)}, u32[]{:S(2)}) async-start(bf16[16,12,7168]{2,1,0:T(8,128)(2,1)} %convert_element_type.66), calls=%async_computation.1 | async-start | bytes 7340032 | tf_op jit(solution)/shard_map/all_to_all | solution.py:125
where the time goes:
time: 296 us; the launch traced here: 294 us
  waiting for transfers between devices  162 us (55%)
  local copies, waits for them, and re-layouts  50.1 us (17%)
  other arithmetic  37.3 us (13%)
  matrix products  33.2 us (11%)
  starting transfers between devices  11.1 us (4%)
    all_to_all x1, waiting for transfers between devices, per_device(): lax.all_to_all(results, 'exp', split_axis=0, concat_axis=0, tiled=True)  81.3 us
    all_to_all x1, waiting for transfers between devices, per_device(): lax.all_to_all(outgoing, 'exp', split_axis=0, concat_axis=0, tiled=True)  81.2 us
    scatter-add x1, other arithmetic, share_partial(): placed = jnp.zeros((row_count, model_width // 128, 128), jnp.float32).at[...  32.7 us
    another operation x2, local copies, waits for them, and re-layouts, hidden_units(): incoming.reshape(row_count, blocks, 128)  9.95 us
    gather x1, local copies, waits for them, and re-layouts, per_device(): gathered = returned[own_targets.reshape(tok_count, choose)]  6.75 us
    dot_general x1, matrix products, hidden_units(): jnp.einsum('rfkc,fkch->rfh', picked, gate_tiles * tile_keep, preferred_el...  6.68 us
    dot_general x1, matrix products, share_partial(): jnp.einsum('rfh,fkhc->rfkc', hidden_part.reshape(row_count, count_blocks,...  6.44 us
    all_to_all x1, starting transfers between devices, per_device(): lax.all_to_all(outgoing, 'exp', split_axis=0, concat_axis=0, tiled=True)  6.29 us
  transfers between devices with their start and end apart: 2, of which 2 were waited for; matrix products, arithmetic and copies ran while one was open for 0% of the time, Pallas kernels for 0%

commit v1 on v0

--- a/solution.py
+++ b/solution.py
@@ -1,7 +1,539 @@
+import functools
+
 import jax
 import jax.numpy as jnp
 from jax import lax
+from jax.experimental import pallas as pl
+from jax.experimental.pallas import tpu as pltpu
 from jax.sharding import PartitionSpec as P
+
+LANES = 128
+
+
+def fused_kernel(
+    nz,
+    tokens_ref,
+    weight_ref,
+    meta_ref,
+    gate_hbm,
+    up_hbm,
+    down_hbm,
+    first_hbm,
+    lift_hbm,
+    squeeze_hbm,
+    last_hbm,
+    out_ref,
+    tok,
+    columns,
+    gate_v,
+    up_v,
+    down_v,
+    first_v,
+    lift_v,
+    squeeze_v,
+    last_v,
+    hidden,
+    segment,
+    part,
+    scale,
+    from_core,
+    from_x,
+    from_low,
+    from_high,
+    to_x,
+    to_z,
+    acc,
+    weight_sem,
+    gz_recv,
+    gx_recv,
+    gc_recv,
+    gup_send,
+    gdown_send,
+    gx_send,
+    gc_send,
+    rc_recv,
+    rx_recv,
+    rlow_recv,
+    rhigh_recv,
+    rc_send,
+    rx_send,
+    rz_send,
+):
+    rows, width = tokens_ref.shape
+    blocks = width // LANES
+    pairs = gate_v.shape[0]
+    count_blocks = hidden.shape[0]
+    per_block = pairs // count_blocks
+    all_rows = tok.shape[0]
+    me = lax.axis_index("exp")
+    core = lax.rem(me, 2)
+    x = lax.rem(me // 2, 2)
+    z = me // 4
+
+    def place(pz, px, pc):
+        return (pz * 2 + px) * 2 + pc
+
+    core_peer = place(z, x, 1 - core)
+    x_peer = place(z, 1 - x, core)
+    up_peer = me + 4
+    down_peer = me - 4
+    has_up = z < nz - 1
+    has_down = z > 0
+
+    def fetch(position, source, target):
+        return pltpu.make_async_copy(source, target, weight_sem.at[position])
+
+    fetches = [
+        fetch(0, first_hbm, first_v),
+        fetch(1, gate_hbm, gate_v),
+        fetch(2, up_hbm, up_v),
+        fetch(3, lift_hbm, lift_v),
+        fetch(4, down_hbm, down_v),
+        fetch(5, squeeze_hbm, squeeze_v),
+        fetch(6, last_hbm, last_v),
+    ]
+
+    barrier = pltpu.get_barrier_semaphore()
+
+    def greet(peer):
+        pl.semaphore_signal(
+            barrier, inc=1, device_id={"exp": peer}, device_id_type=pl.DeviceIdType.MESH
+        )
+
+    greet(core_peer)
+    greet(x_peer)
+
+    @pl.when(has_up)
+    def _():
+        greet(up_peer)
+
+    @pl.when(has_down)
+    def _():
+        greet(down_peer)
+
+    own_rows = pl.ds(pl.multiple_of(me * rows, rows), rows)
+    tok[own_rows, :width] = tokens_ref[...]
+    weights = weight_ref[...]
+    lane = lax.broadcasted_iota(jnp.int32, weights.shape, 1)
+    high = weights.astype(jnp.bfloat16)
+    rest = weights - high.astype(jnp.float32)
+    middle = rest.astype(jnp.bfloat16)
+    low_part = rest - middle.astype(jnp.float32)
+    experts = 4 * nz
+    tok[own_rows, width:] = jnp.where(
+        lane < experts,
+        high.astype(jnp.float32),
+        jnp.where(lane < 2 * experts, middle.astype(jnp.float32), low_part),
+    ).astype(jnp.bfloat16)
+
+    degree = 2 + has_up.astype(jnp.int32) + has_down.astype(jnp.int32)
+    pl.semaphore_wait(barrier, degree)
+
+    def remote(source, target, send, recv, peer):
+        return pltpu.make_async_remote_copy(
+            src_ref=source,
+            dst_ref=target,
+            send_sem=send,
+            recv_sem=recv,
+            device_id={"exp": peer},
+            device_id_type=pl.DeviceIdType.MESH,
+        )
+
+    def block_of(pz, px, pc):
+        return tok.at[pl.ds(pl.multiple_of(place(pz, px, pc) * rows, rows), rows)]
+
+    def g_up(pz):
+        b = block_of(pz, x, core)
+        return remote(b, b, gup_send.at[pz], gz_recv.at[pz], up_peer)
+
+    def g_down(pz):
+        b = block_of(pz, x, core)
+        return remote(b, b, gdown_send.at[pz], gz_recv.at[pz], down_peer)
+
+    def g_x(pz, px):
+        b = block_of(pz, px, core)
+        return remote(b, b, gx_send.at[pz], gx_recv.at[pz], x_peer)
+
+    def g_core(pz, px, pc):
+        b = block_of(pz, px, pc)
+        return remote(b, b, gc_send.at[pz, px], gc_recv.at[pz, px], core_peer)
+
+    def both_sides(distance, act):
+        @pl.when(z >= distance)
+        def _():
+            act(z - distance, True)
+
+        @pl.when(z + distance < nz)
+        def _():
+            act(z + distance, False)
+
+    def spread_x(pz):
+        g_x(pz, x).start()
+        g_core(pz, x, core).start()
+
+    def pass_on(pz, upward):
+        if upward:
+            g_up(pz).wait_recv()
+
+            @pl.when(has_up)
+            def _():
+                g_up(pz).start()
+        else:
+            g_down(pz).wait_recv()
+
+            @pl.when(has_down)
+            def _():
+                g_down(pz).start()
+        spread_x(pz)
+
+    def cross(pz, upward=True):
+        g_x(pz, 1 - x).wait_recv()
+        g_core(pz, 1 - x, core).start()
+
+    @pl.when(has_up)
+    def _():
+        g_up(z).start()
+
+    @pl.when(has_down)
+    def _():
+        g_down(z).start()
+
+    spread_x(z)
+    for one in fetches:
+        one.start()
+    for distance in range(1, nz):
+        both_sides(distance, pass_on)
+        if distance == 1:
+            cross(z)
+        else:
+            both_sides(distance - 1, cross)
+    both_sides(nz - 1, cross)
+    for pz in range(nz):
+        for px in range(2):
+            g_core(pz, px, 1 - core).wait_recv()
+    for pz in range(nz):
+
+        @pl.when(jnp.logical_and(has_up, pz <= z))
+        def _():
+            g_up(pz).wait_send()
+
+        @pl.when(jnp.logical_and(has_down, pz >= z))
+        def _():
+            g_down(pz).wait_send()
+
+        g_x(pz, x).wait_send()
+        for px in range(2):
+            g_core(pz, px, core).wait_send()
+
+    sent = tok[:, width:].astype(jnp.float32)
+    lane = lax.broadcasted_iota(jnp.int32, sent.shape, 1)
+    mine = jnp.logical_and(lax.rem(lane, experts) == me, lane < 3 * experts)
+    column = jnp.sum(jnp.where(mine, sent, 0.0), axis=1, keepdims=True)
+    scale[...] = jnp.broadcast_to(column, scale.shape)
+
+    fetches[0].wait()
+    depth = 8 * LANES if blocks % 8 == 0 else LANES
+
+    def column_step(d, carry):
+        columns[d] = tok[:, pl.ds(pl.multiple_of(d * LANES, LANES), LANES)]
+        return carry
+
+    lax.fori_loop(0, blocks, column_step, 0)
+
+    def low_step(step, total):
+        at = pl.ds(pl.multiple_of(step * depth, depth), depth)
+        return total + jnp.dot(tok[:, at], first_v[at, :], preferred_element_type=jnp.float32)
+
+    low = lax.fori_loop(
+        0, width // depth, low_step, jnp.zeros((all_rows, LANES), jnp.float32)
+    ).astype(jnp.bfloat16)
+    for one in fetches[1:4]:
+        one.wait()
+
+    def keep_tile(value):
+        some = jnp.full((16, LANES), value.astype(jnp.float32)).astype(jnp.bfloat16)
+        return jnp.concatenate([some] * (LANES // 16), axis=0)
+
+    def hidden_step(f, carry):
+        left, right = [], []
+        for k in range(per_block):
+            pair = f * per_block + k
+            left.append(columns[meta_ref[0, pair]])
+            keep = keep_tile(meta_ref[1, pair])
+            right.append(jnp.concatenate([gate_v[pair] * keep, up_v[pair] * keep], axis=1))
+        units = pl.ds(pl.multiple_of(f * LANES, LANES), LANES)
+        left.append(low)
+        right.append(jnp.concatenate([lift_v[0, :, units], lift_v[1, :, units]], axis=1))
+        both = jnp.dot(
+            jnp.concatenate(left, axis=1),
+            jnp.concatenate(right, axis=0),
+            preferred_element_type=jnp.float32,
+        )
+        gate, up = both[:, :LANES], both[:, LANES:]
+        hidden[f] = (gate / (1.0 + jnp.exp(-gate)) * up).astype(jnp.bfloat16)
+        return carry
+
+    lax.fori_loop(0, count_blocks, hidden_step, 0)
+    for one in fetches[4:]:
+        one.wait()
+
+    def squeeze_step(f, total):
+        at = pl.ds(pl.multiple_of(f * LANES, LANES), LANES)
+        return total + jnp.dot(hidden[f], squeeze_v[at, :], preferred_element_type=jnp.float32)
+
+    squeezed = lax.fori_loop(
+        0, count_blocks, squeeze_step, jnp.zeros((all_rows, LANES), jnp.float32)
+    ).astype(jnp.bfloat16)
+
+    def down_step(step, total):
+        pair = meta_ref[2, step]
+        tile = down_v[pair] * keep_tile(meta_ref[4, step])
+        again = meta_ref[5, step].astype(jnp.float32)
+        total = total * again + jnp.dot(
+            hidden[meta_ref[3, step]], tile, preferred_element_type=jnp.float32
+        )
+        segment[step] = total
+        return total
+
+    lax.fori_loop(0, pairs, down_step, jnp.zeros((all_rows, LANES), jnp.float32))
+
+    def output_step(d, carry):
+        at = pl.ds(pl.multiple_of(d * LANES, LANES), LANES)
+        value = jnp.dot(squeezed, last_v[:, at], preferred_element_type=jnp.float32)
+        value = value + segment[meta_ref[6, d]] * meta_ref[7, d].astype(jnp.float32)
+        value = value.astype(jnp.bfloat16).astype(jnp.float32) * scale[...]
+        part[:, at] = value.astype(jnp.bfloat16)
+        return carry
+
+    lax.fori_loop(0, blocks, output_step, 0)
+
+    def part_of(pz, px, pc):
+        return part.at[pl.ds(pl.multiple_of(place(pz, px, pc) * rows, rows), rows)]
+
+    def r_core(pz, px):
+        return remote(
+            part_of(pz, px, 1 - core),
+            from_core.at[pz, px],
+            rc_send.at[pz, px],
+            rc_recv.at[pz, px],
+            core_peer,
+        )
+
+    def r_x(pz):
+        return remote(to_x.at[pz], from_x.at[pz], rx_send.at[pz], rx_recv.at[pz], x_peer)
+
+    def r_up(pz):
+        return remote(to_z.at[pz], from_low.at[pz], rz_send.at[pz], rlow_recv.at[pz], up_peer)
+
+    def r_down(pz):
+        return remote(to_z.at[pz], from_high.at[pz], rz_send.at[pz], rhigh_recv.at[pz], down_peer)
+
+    def wide(value):
+        return value.astype(jnp.float32)
+
+    def ordered(act):
+        for distance in range(nz - 1, 0, -1):
+            both_sides(distance, act)
+
+    def core_start(pz, px):
+        r_core(pz, px).start()
+
+    ordered(lambda pz, lower: core_start(pz, 1 - x))
+    core_start(z, 1 - x)
+    ordered(lambda pz, lower: core_start(pz, x))
+    core_start(z, x)
+
+    def x_start(pz, lower=True):
+        r_core(pz, 1 - x).wait_recv()
+        total = wide(part_of(pz, 1 - x, core)[...]) + wide(from_core[pz, 1 - x])
+        to_x[pz] = total.astype(jnp.bfloat16)
+        r_x(pz).start()
+
+    ordered(x_start)
+    x_start(z)
+
+    def local_sum(pz):
+        r_core(pz, x).wait_recv()
+        r_x(pz).wait_recv()
+        total = wide(part_of(pz, x, core)[...]) + wide(from_core[pz, x])
+        return total + wide(from_x[pz])
+
+    def z_step(pz, lower):
+        acc[...] = local_sum(pz)
+        if lower:
+
+            @pl.when(has_up)
+            def _():
+                r_down(pz).wait_recv()
+                acc[...] += wide(from_high[pz])
+
+            to_z[pz] = acc[...].astype(jnp.bfloat16)
+            r_down(pz).start()
+        else:
+
+            @pl.when(has_down)
+            def _():
+                r_up(pz).wait_recv()
+                acc[...] += wide(from_low[pz])
+
+            to_z[pz] = acc[...].astype(jnp.bfloat16)
+            r_up(pz).start()
+
+    ordered(z_step)
+    acc[...] = local_sum(z)
+
+    @pl.when(has_up)
+    def _():
+        r_down(z).wait_recv()
+        acc[...] += wide(from_high[z])
+
+    @pl.when(has_down)
+    def _():
+        r_up(z).wait_recv()
+        acc[...] += wide(from_low[z])
+
+    out_ref[...] = acc[...].astype(jnp.bfloat16)
+
+    for pz in range(nz):
+        r_x(pz).wait_send()
+        for px in range(2):
+            r_core(pz, px).wait_send()
+
+        @pl.when(pz != z)
+        def _():
+            r_up(pz).wait_send()
+
+
+def tile_plan(base_index, keep, blocks):
+    flat = base_index.reshape(-1)
+    pairs = flat.shape[0]
+    place = jnp.arange(pairs, dtype=jnp.int32)
+    ahead = (flat[:, None] < flat[None, :]) | (
+        (flat[:, None] == flat[None, :]) & (place[:, None] < place[None, :])
+    )
+    rank = jnp.sum(ahead.astype(jnp.int32), axis=0)
+    chosen = (rank[:, None] == place[None, :]).astype(jnp.int32)
+    keep = keep.reshape(-1)
+    order = jnp.sum(chosen * place[:, None], axis=0)
+    sorted_keep = jnp.sum(chosen * keep[:, None], axis=0)
+    sorted_block = jnp.sum(chosen * flat[:, None], axis=0)
+    again = jnp.concatenate(
+        [jnp.zeros((1,), jnp.int32), (sorted_block[1:] == sorted_block[:-1]).astype(jnp.int32)]
+    )
+    block = jnp.arange(blocks, dtype=jnp.int32)
+    upto = jnp.sum((flat[:, None] <= block[None, :]).astype(jnp.int32), axis=0)
+    used = jnp.any(flat[:, None] == block[None, :], axis=0).astype(jnp.int32)
+    size = max(pairs, blocks)
+
+    def row(values):
+        return jnp.pad(values, (0, size - values.shape[0]))
+
+    return jnp.stack(
+        [
+            row(flat),
+            row(keep),
+            row(order),
+            row(order // base_index.shape[1]),
+            row(sorted_keep),
+            row(again),
+            row(jnp.maximum(upto - 1, 0)),
+            row(used),
+        ]
+    )
+
+
+def per_device_fused(
+    tokens,
+    routes,
+    route_weight,
+    base_index,
+    expert_mask,
+    base_gate,
+    base_up,
+    base_down,
+    delta_in,
+    delta_gate_up,
+    delta_down_in,
+    delta_out,
+):
+    rows, width = tokens.shape
+    experts = lax.axis_size("exp")
+    nz = experts // 4
+    blocks = width // LANES
+    count_blocks, per_block = base_index.shape
+    pairs = count_blocks * per_block
+    all_rows = rows * experts
+    named = routes[:, :, None] == jnp.arange(experts, dtype=jnp.int32)[None, None, :]
+    weights = jnp.sum(jnp.where(named, route_weight[:, :, None], 0.0), axis=1)
+    weights = jnp.pad(
+        jnp.concatenate([weights] * 3, axis=1), ((0, 0), (0, LANES - 3 * experts))
+    )
+    meta = tile_plan(base_index, expert_mask[0], blocks)
+    lift = delta_gate_up[0]
+    units = lift.shape[2]
+    bf16, f32 = jnp.bfloat16, jnp.float32
+    vmem, smem, anywhere = (
+        pl.BlockSpec(memory_space=space) for space in (pltpu.VMEM, pltpu.SMEM, pl.ANY)
+    )
+    dma = pltpu.SemaphoreType.DMA
+    return pl.pallas_call(
+        functools.partial(fused_kernel, nz),
+        out_shape=jax.ShapeDtypeStruct((rows, width), bf16),
+        in_specs=[vmem, vmem, smem] + [anywhere] * 7,
+        out_specs=vmem,
+        scratch_shapes=[
+            pltpu.VMEM((all_rows, width + LANES), bf16),
+            pltpu.VMEM((blocks, all_rows, LANES), bf16),
+            pltpu.VMEM((pairs, LANES, LANES), bf16),
+            pltpu.VMEM((pairs, LANES, LANES), bf16),
+            pltpu.VMEM((pairs, LANES, LANES), bf16),
+            pltpu.VMEM((width, LANES), bf16),
+            pltpu.VMEM((2, LANES, units), bf16),
+            pltpu.VMEM((units, LANES), bf16),
+            pltpu.VMEM((LANES, width), bf16),
+            pltpu.VMEM((count_blocks, all_rows, LANES), bf16),
+            pltpu.VMEM((pairs, all_rows, LANES), f32),
+            pltpu.VMEM((all_rows, width), bf16),
+            pltpu.VMEM((all_rows, LANES), f32),
+            pltpu.VMEM((nz, 2, rows, width), bf16),
+            pltpu.VMEM((nz, rows, width), bf16),
+            pltpu.VMEM((nz, rows, width), bf16),
+            pltpu.VMEM((nz, rows, width), bf16),
+            pltpu.VMEM((nz, rows, width), bf16),
+            pltpu.VMEM((nz, rows, width), bf16),
+            pltpu.VMEM((rows, width), f32),
+            dma((7,)),
+            dma((nz,)),
+            dma((nz,)),
+            dma((nz, 2)),
+            dma((nz,)),
+            dma((nz,)),
+            dma((nz,)),
+            dma((nz, 2)),
+            dma((nz, 2)),
+            dma((nz,)),
+            dma((nz,)),
+            dma((nz,)),
+            dma((nz, 2)),
+            dma((nz,)),
+            dma((nz,)),
+        ],
+        compiler_params=pltpu.CompilerParams(
+            collective_id=0, has_side_effects=True, vmem_limit_bytes=60 << 20
+        ),
+        name="expert_layer",
+    )(
+        tokens,
+        weights,
+        meta,
+        base_gate.reshape(pairs, LANES, LANES),
+        base_up.reshape(pairs, LANES, LANES),
+        base_down.reshape(pairs, LANES, LANES),
+        delta_in[0],
+        lift,
+        delta_down_in[0],
+        delta_out[0],
+    )
 
 
 def place_rows(route_block, experts, most_rows, copies, copy_index):
@@ -131,8 +663,9 @@
 
 
 def solution(mesh):
+    small = mesh.shape["base"] == 1 and mesh.shape["exp"] == 16
     return jax.shard_map(
-        per_device,
+        per_device_fused if small else per_device,
         mesh=mesh,
         in_specs=(
             P(("groups", "exp", "base"), None),

time: 296 us -> 103 us (0.35)
  the two profiles are of different devices: /device:TPU:16 before, /device:TPU:0 now
where the time goes in v1:
time: 103 us
  Pallas kernels  95.9 us (93%)
  local copies, waits for them, and re-layouts  5.63 us (5%)
  other arithmetic  1.4 us (1%)
    pallas_call x1, Pallas kernels, per_device_fused(): pl.pallas_call(functools.partial(fused_kernel, nz), out_shape=jax.ShapeDt...  95.9 us
    unnamed x5, local copies, waits for them, and re-layouts  4.67 us

profile of v1, /device:TPU:0, one launch (start us, length us, event | category | flops | bytes accessed | tf_op | source)
XLA Modules:
  0.0 103.0 jit_solution(17031188638377147773)
XLA Ops:
  0.0 0.8 copy.27
  0.8 0.1 lt.32
  0.8 0.1 stack.31
  0.9 0.1 fusion.2
  1.1 0.1 convert_reduce_fusion.1
  1.2 0.1 convert_reduce_fusion
  1.3 0.8 copy.28
  2.1 0.1 mul.11
  2.1 0.1 stack.32
  2.2 0.1 select_reduce_fusion
  2.4 0.1 slice_compare_fusion
  2.4 0.1 fusion.3
  2.5 0.6 stack.40.meta_ref
  3.1 0.8 copy.25
  3.9 0.8 copy.26
  4.7 0.1 select_reduce_fusion.3
  4.8 0.7 select_maximum_fusion.weight_ref
  5.4 95.9 %expert_layer.1 = bf16[16,7168]{1,0:T(8,128)(2,1)} custom-call(bf16[16,7168]{1,0:T(8,128)(2,1)} %tokens_ref.1, f32[16,128]{1,0:T(8,128)} %select_maximum_fusion.weight_ref, s32[8,128]{1,0:T(8,128)} %stack.40.meta_ref, bf16[128,128,128]{2,1,0:T(8,128)(2,1)} %bitcast.16, bf16[128,128,128]{2,1,0:T(8,128)(2,1)} %bitcast.17, bf16[128,128,128]{2,1,0:T(8,128)(2,1)} %bitcast.18, ...), custom_call_target="tpu_custom_call" | custom-call | tf_op jit(solution)/shard_map/expert_layer/pallas_call | solution.py:479
  101.3 1.6 %copy.32 = bf16[16,7168]{1,0:T(8,128)(2,1)} copy(bf16[16,7168]{1,0:T(8,128)(2,1)} %expert_layer.1) | data formatting | bytes 458752
  (3 shorter events, 0.0 us)

commit v2 on v1

--- a/solution.py
+++ b/solution.py
@@ -201,111 +201,121 @@
     spread_x(z)
     for one in fetches:
         one.start()
-    for distance in range(1, nz):
+    half_rows = all_rows // 2
+    own_half = z // (nz // 2)
+    other_half = 1 - own_half
+
+    def half_at(half):
+        return pl.ds(pl.multiple_of(half * half_rows, half_rows), half_rows)
+
+    def core_arrived(half):
+        for step in range(nz // 2):
+            for px in range(2):
+                g_core(half * (nz // 2) + step, px, 1 - core).wait_recv()
+
+    depth = 8 * LANES if blocks % 8 == 0 else LANES
+
+    def keep_tile(value):
+        some = jnp.full((16, LANES), value.astype(jnp.float32)).astype(jnp.bfloat16)
+        return jnp.concatenate([some] * (LANES // 16), axis=0)
+
+    def compute_hidden(half):
+        at_rows = half_at(half)
+        sent = tok[at_rows, width:].astype(jnp.float32)
+        lane = lax.broadcasted_iota(jnp.int32, sent.shape, 1)
+        mine = jnp.logical_and(lax.rem(lane, experts) == me, lane < 3 * experts)
+        column = jnp.sum(jnp.where(mine, sent, 0.0), axis=1, keepdims=True)
+        scale[...] = jnp.broadcast_to(column, scale.shape)
+
+        def column_step(d, carry):
+            columns[d] = tok[at_rows, pl.ds(pl.multiple_of(d * LANES, LANES), LANES)]
+            return carry
+
+        lax.fori_loop(0, blocks, column_step, 0, unroll=4)
+
+        def low_step(step, total):
+            at = pl.ds(pl.multiple_of(step * depth, depth), depth)
+            return total + jnp.dot(
+                tok[at_rows, at], first_v[at, :], preferred_element_type=jnp.float32
+            )
+
+        low = lax.fori_loop(
+            0, width // depth, low_step, jnp.zeros((half_rows, LANES), jnp.float32)
+        ).astype(jnp.bfloat16)
+
+        def hidden_step(f, carry):
+            left, right = [], []
+            for k in range(per_block):
+                pair = f * per_block + k
+                left.append(columns[meta_ref[0, pair]])
+                keep = keep_tile(meta_ref[1, pair])
+                right.append(jnp.concatenate([gate_v[pair] * keep, up_v[pair] * keep], axis=1))
+            units = pl.ds(pl.multiple_of(f * LANES, LANES), LANES)
+            left.append(low)
+            right.append(jnp.concatenate([lift_v[0, :, units], lift_v[1, :, units]], axis=1))
+            both = jnp.dot(
+                jnp.concatenate(left, axis=1),
+                jnp.concatenate(right, axis=0),
+                preferred_element_type=jnp.float32,
+            )
+            gate, up = both[:, :LANES], both[:, LANES:]
+            hidden[f] = (gate / (1.0 + jnp.exp(-gate)) * up).astype(jnp.bfloat16)
+            return carry
+
+        lax.fori_loop(0, count_blocks, hidden_step, 0, unroll=2)
+
+    def compute_part(half):
+        at_rows = half_at(half)
+
+        def squeeze_step(f, total):
+            at = pl.ds(pl.multiple_of(f * LANES, LANES), LANES)
+            return total + jnp.dot(hidden[f], squeeze_v[at, :], preferred_element_type=jnp.float32)
+
+        squeezed = lax.fori_loop(
+            0, count_blocks, squeeze_step, jnp.zeros((half_rows, LANES), jnp.float32), unroll=8
+        ).astype(jnp.bfloat16)
+
+        def down_step(step, total):
+            pair = meta_ref[2, step]
+            tile = down_v[pair] * keep_tile(meta_ref[4, step])
+            again = meta_ref[5, step].astype(jnp.float32)
+            total = total * again + jnp.dot(
+                hidden[meta_ref[3, step]], tile, preferred_element_type=jnp.float32
+            )
+            segment[step] = total
+            return total
+
+        lax.fori_loop(
+            0, pairs, down_step, jnp.zeros((half_rows, LANES), jnp.float32), unroll=8
+        )
+
+        def output_step(d, carry):
+            at = pl.ds(pl.multiple_of(d * LANES, LANES), LANES)
+            value = jnp.dot(squeezed, last_v[:, at], preferred_element_type=jnp.float32)
+            value = value + segment[meta_ref[6, d]] * meta_ref[7, d].astype(jnp.float32)
+            value = value.astype(jnp.bfloat16).astype(jnp.float32) * scale[...]
+            part[at_rows, at] = value.astype(jnp.bfloat16)
+            return carry
+
+        lax.fori_loop(0, blocks, output_step, 0, unroll=4)
+
+    for distance in range(1, nz - 1):
         both_sides(distance, pass_on)
         if distance == 1:
             cross(z)
         else:
             both_sides(distance - 1, cross)
-    both_sides(nz - 1, cross)
-    for pz in range(nz):
-        for px in range(2):
-            g_core(pz, px, 1 - core).wait_recv()
-    for pz in range(nz):
-
-        @pl.when(jnp.logical_and(has_up, pz <= z))
-        def _():
-            g_up(pz).wait_send()
-
-        @pl.when(jnp.logical_and(has_down, pz >= z))
-        def _():
-            g_down(pz).wait_send()
-
-        g_x(pz, x).wait_send()
-        for px in range(2):
-            g_core(pz, px, core).wait_send()
-
-    sent = tok[:, width:].astype(jnp.float32)
-    lane = lax.broadcasted_iota(jnp.int32, sent.shape, 1)
-    mine = jnp.logical_and(lax.rem(lane, experts) == me, lane < 3 * experts)
-    column = jnp.sum(jnp.where(mine, sent, 0.0), axis=1, keepdims=True)
-    scale[...] = jnp.broadcast_to(column, scale.shape)
-
-    fetches[0].wait()
-    depth = 8 * LANES if blocks % 8 == 0 else LANES
-
-    def column_step(d, carry):
-        columns[d] = tok[:, pl.ds(pl.multiple_of(d * LANES, LANES), LANES)]
-        return carry
-
-    lax.fori_loop(0, blocks, column_step, 0)
-
-    def low_step(step, total):
-        at = pl.ds(pl.multiple_of(step * depth, depth), depth)
-        return total + jnp.dot(tok[:, at], first_v[at, :], preferred_element_type=jnp.float32)
-
-    low = lax.fori_loop(
-        0, width // depth, low_step, jnp.zeros((all_rows, LANES), jnp.float32)
-    ).astype(jnp.bfloat16)
-    for one in fetches[1:4]:
+    core_arrived(own_half)
+    for one in fetches[:4]:
         one.wait()
-
-    def keep_tile(value):
-        some = jnp.full((16, LANES), value.astype(jnp.float32)).astype(jnp.bfloat16)
-        return jnp.concatenate([some] * (LANES // 16), axis=0)
-
-    def hidden_step(f, carry):
-        left, right = [], []
-        for k in range(per_block):
-            pair = f * per_block + k
-            left.append(columns[meta_ref[0, pair]])
-            keep = keep_tile(meta_ref[1, pair])
-            right.append(jnp.concatenate([gate_v[pair] * keep, up_v[pair] * keep], axis=1))
-        units = pl.ds(pl.multiple_of(f * LANES, LANES), LANES)
-        left.append(low)
-        right.append(jnp.concatenate([lift_v[0, :, units], lift_v[1, :, units]], axis=1))
-        both = jnp.dot(
-            jnp.concatenate(left, axis=1),
-            jnp.concatenate(right, axis=0),
-            preferred_element_type=jnp.float32,
-        )
-        gate, up = both[:, :LANES], both[:, LANES:]
-        hidden[f] = (gate / (1.0 + jnp.exp(-gate)) * up).astype(jnp.bfloat16)
-        return carry
-
-    lax.fori_loop(0, count_blocks, hidden_step, 0)
+    compute_hidden(own_half)
+    both_sides(nz - 1, pass_on)
+    both_sides(nz - 2, cross)
     for one in fetches[4:]:
         one.wait()
-
-    def squeeze_step(f, total):
-        at = pl.ds(pl.multiple_of(f * LANES, LANES), LANES)
-        return total + jnp.dot(hidden[f], squeeze_v[at, :], preferred_element_type=jnp.float32)
-
-    squeezed = lax.fori_loop(
-        0, count_blocks, squeeze_step, jnp.zeros((all_rows, LANES), jnp.float32)
-    ).astype(jnp.bfloat16)
-
-    def down_step(step, total):
-        pair = meta_ref[2, step]
-        tile = down_v[pair] * keep_tile(meta_ref[4, step])
-        again = meta_ref[5, step].astype(jnp.float32)
-        total = total * again + jnp.dot(
-            hidden[meta_ref[3, step]], tile, preferred_element_type=jnp.float32
-        )
-        segment[step] = total
-        return total
-
-    lax.fori_loop(0, pairs, down_step, jnp.zeros((all_rows, LANES), jnp.float32))
-
-    def output_step(d, carry):
-        at = pl.ds(pl.multiple_of(d * LANES, LANES), LANES)
-        value = jnp.dot(squeezed, last_v[:, at], preferred_element_type=jnp.float32)
-        value = value + segment[meta_ref[6, d]] * meta_ref[7, d].astype(jnp.float32)
-        value = value.astype(jnp.bfloat16).astype(jnp.float32) * scale[...]
-        part[:, at] = value.astype(jnp.bfloat16)
-        return carry
-
-    lax.fori_loop(0, blocks, output_step, 0)
+    compute_part(own_half)
+    both_sides(nz - 1, cross)
+    core_arrived(other_half)
 
     def part_of(pz, px, pc):
         return part.at[pl.ds(pl.multiple_of(place(pz, px, pc) * rows, rows), rows)]
@@ -338,19 +348,32 @@
     def core_start(pz, px):
         r_core(pz, px).start()
 
-    ordered(lambda pz, lower: core_start(pz, 1 - x))
+    mate = own_half * nz + nz // 2 - 1 - z
+
+    def other_side(act):
+        near = jnp.where(own_half == 0, nz // 2, nz // 2 - 1)
+        toward = 1 - 2 * own_half
+        for step in range(nz // 2 - 1, -1, -1):
+            act(near + toward * step)
+
+    core_start(mate, 1 - x)
     core_start(z, 1 - x)
-    ordered(lambda pz, lower: core_start(pz, x))
+    core_start(mate, x)
     core_start(z, x)
-
-    def x_start(pz, lower=True):
+    compute_hidden(other_half)
+
+    def x_start(pz):
         r_core(pz, 1 - x).wait_recv()
         total = wide(part_of(pz, 1 - x, core)[...]) + wide(from_core[pz, 1 - x])
         to_x[pz] = total.astype(jnp.bfloat16)
         r_x(pz).start()
 
-    ordered(x_start)
+    x_start(mate)
     x_start(z)
+    compute_part(other_half)
+    other_side(lambda pz: core_start(pz, 1 - x))
+    other_side(lambda pz: core_start(pz, x))
+    other_side(x_start)
 
     def local_sum(pz):
         r_core(pz, x).wait_recv()
@@ -402,6 +425,20 @@
         @pl.when(pz != z)
         def _():
             r_up(pz).wait_send()
+
+    for pz in range(nz):
+
+        @pl.when(jnp.logical_and(has_up, pz <= z))
+        def _():
+            g_up(pz).wait_send()
+
+        @pl.when(jnp.logical_and(has_down, pz >= z))
+        def _():
+            g_down(pz).wait_send()
+
+        g_x(pz, x).wait_send()
+        for px in range(2):
+            g_core(pz, px, core).wait_send()
 
 
 def tile_plan(base_index, keep, blocks):
@@ -483,7 +520,7 @@
         out_specs=vmem,
         scratch_shapes=[
             pltpu.VMEM((all_rows, width + LANES), bf16),
-            pltpu.VMEM((blocks, all_rows, LANES), bf16),
+            pltpu.VMEM((blocks, all_rows // 2, LANES), bf16),
             pltpu.VMEM((pairs, LANES, LANES), bf16),
             pltpu.VMEM((pairs, LANES, LANES), bf16),
             pltpu.VMEM((pairs, LANES, LANES), bf16),
@@ -491,10 +528,10 @@
             pltpu.VMEM((2, LANES, units), bf16),
             pltpu.VMEM((units, LANES), bf16),
             pltpu.VMEM((LANES, width), bf16),
-            pltpu.VMEM((count_blocks, all_rows, LANES), bf16),
-            pltpu.VMEM((pairs, all_rows, LANES), f32),
+            pltpu.VMEM((count_blocks, all_rows // 2, LANES), bf16),
+            pltpu.VMEM((pairs, all_rows // 2, LANES), f32),
             pltpu.VMEM((all_rows, width), bf16),
-            pltpu.VMEM((all_rows, LANES), f32),
+            pltpu.VMEM((all_rows // 2, LANES), f32),
             pltpu.VMEM((nz, 2, rows, width), bf16),
             pltpu.VMEM((nz, rows, width), bf16),
             pltpu.VMEM((nz, rows, width), bf16),

time: 103 us -> 79.9 us (0.78)
  Pallas kernels: 95.9 us -> 72.5 us
    pallas_call x1, Pallas kernels: 95.9 us -> 72.5 us  [per_device_fused(): pl.pallas_call(functools.partial(fused_kernel, nz), out_shape=jax.ShapeDt...]
where the time goes in v2:
time: 79.9 us; the launch traced here: 79.6 us
  Pallas kernels  72.5 us (91%)
  local copies, waits for them, and re-layouts  5.63 us (7%)
  other arithmetic  1.4 us (2%)
    pallas_call x1, Pallas kernels, per_device_fused(): pl.pallas_call(functools.partial(fused_kernel, nz), out_shape=jax.ShapeDt...  72.5 us
    unnamed x5, local copies, waits for them, and re-layouts  4.67 us

profile of v2, /device:TPU:0, one launch (start us, length us, event | category | flops | bytes accessed | tf_op | source)
XLA Modules:
  0.0 79.6 jit_solution(1271573188393395436)
XLA Ops:
  0.0 0.8 copy.27
  0.8 0.1 lt.32
  0.8 0.1 stack.31
  0.9 0.1 fusion.2
  1.1 0.1 convert_reduce_fusion.1
  1.2 0.1 convert_reduce_fusion
  1.3 0.8 copy.28
  2.1 0.1 mul.11
  2.1 0.1 stack.32
  2.2 0.1 select_reduce_fusion
  2.4 0.1 slice_compare_fusion
  2.4 0.1 fusion.3
  2.5 0.6 stack.40.meta_ref
  3.1 0.8 copy.25
  3.9 0.8 copy.26
  4.7 0.1 select_reduce_fusion.3
  4.8 0.7 select_maximum_fusion.weight_ref
  5.4 72.5 %expert_layer.1 = bf16[16,7168]{1,0:T(8,128)(2,1)} custom-call(bf16[16,7168]{1,0:T(8,128)(2,1)} %tokens_ref.1, f32[16,128]{1,0:T(8,128)} %select_maximum_fusion.weight_ref, s32[8,128]{1,0:T(8,128)} %stack.40.meta_ref, bf16[128,128,128]{2,1,0:T(8,128)(2,1)} %bitcast.16, bf16[128,128,128]{2,1,0:T(8,128)(2,1)} %bitcast.17, bf16[128,128,128]{2,1,0:T(8,128)(2,1)} %bitcast.18, ...), custom_call_target="tpu_custom_call" | custom-call | tf_op jit(solution)/shard_map/expert_layer/pallas_call | solution.py:516
  78.0 1.6 %copy.32 = bf16[16,7168]{1,0:T(8,128)(2,1)} copy(bf16[16,7168]{1,0:T(8,128)(2,1)} %expert_layer.1) | data formatting | bytes 458752
  (3 shorter events, 0.0 us)

commit v3 on v2

--- a/solution.py
+++ b/solution.py
@@ -12,6 +12,8 @@
 
 def fused_kernel(
     nz,
+    gather_cuts,
+    reduce_cuts,
     tokens_ref,
     weight_ref,
     meta_ref,
@@ -139,24 +141,29 @@
             device_id_type=pl.DeviceIdType.MESH,
         )
 
-    def block_of(pz, px, pc):
-        return tok.at[pl.ds(pl.multiple_of(place(pz, px, pc) * rows, rows), rows)]
-
-    def g_up(pz):
-        b = block_of(pz, x, core)
-        return remote(b, b, gup_send.at[pz], gz_recv.at[pz], up_peer)
-
-    def g_down(pz):
-        b = block_of(pz, x, core)
-        return remote(b, b, gdown_send.at[pz], gz_recv.at[pz], down_peer)
-
-    def g_x(pz, px):
-        b = block_of(pz, px, core)
-        return remote(b, b, gx_send.at[pz], gx_recv.at[pz], x_peer)
-
-    def g_core(pz, px, pc):
-        b = block_of(pz, px, pc)
-        return remote(b, b, gc_send.at[pz, px], gc_recv.at[pz, px], core_peer)
+    all_blocks = blocks + 1
+    edges = [(part * all_blocks // gather_cuts) * LANES for part in range(gather_cuts + 1)]
+    gather_parts = range(gather_cuts)
+
+    def block_of(pz, px, pc, cut):
+        at = pl.ds(pl.multiple_of(place(pz, px, pc) * rows, rows), rows)
+        return tok.at[at, pl.ds(edges[cut], edges[cut + 1] - edges[cut])]
+
+    def g_up(pz, cut):
+        b = block_of(pz, x, core, cut)
+        return remote(b, b, gup_send.at[pz, cut], gz_recv.at[pz, cut], up_peer)
+
+    def g_down(pz, cut):
+        b = block_of(pz, x, core, cut)
+        return remote(b, b, gdown_send.at[pz, cut], gz_recv.at[pz, cut], down_peer)
+
+    def g_x(pz, px, cut):
+        b = block_of(pz, px, core, cut)
+        return remote(b, b, gx_send.at[pz, cut], gx_recv.at[pz, cut], x_peer)
+
+    def g_core(pz, px, pc, cut):
+        b = block_of(pz, px, pc, cut)
+        return remote(b, b, gc_send.at[pz, px, cut], gc_recv.at[pz, px, cut], core_peer)
 
     def both_sides(distance, act):
         @pl.when(z >= distance)
@@ -167,38 +174,46 @@
         def _():
             act(z + distance, False)
 
-    def spread_x(pz):
-        g_x(pz, x).start()
-        g_core(pz, x, core).start()
-
-    def pass_on(pz, upward):
+    def spread_x(pz, cut):
+        g_x(pz, x, cut).start()
+        g_core(pz, x, core, cut).start()
+
+    def pass_on(cut, pz, upward):
         if upward:
-            g_up(pz).wait_recv()
+            g_up(pz, cut).wait_recv()
 
             @pl.when(has_up)
             def _():
-                g_up(pz).start()
+                g_up(pz, cut).start()
         else:
-            g_down(pz).wait_recv()
+            g_down(pz, cut).wait_recv()
 
             @pl.when(has_down)
             def _():
-                g_down(pz).start()
-        spread_x(pz)
-
-    def cross(pz, upward=True):
-        g_x(pz, 1 - x).wait_recv()
-        g_core(pz, 1 - x, core).start()
-
-    @pl.when(has_up)
-    def _():
-        g_up(z).start()
-
-    @pl.when(has_down)
-    def _():
-        g_down(z).start()
-
-    spread_x(z)
+                g_down(pz, cut).start()
+        spread_x(pz, cut)
+
+    def cross(cut, pz, upward=True):
+        g_x(pz, 1 - x, cut).wait_recv()
+        g_core(pz, 1 - x, core, cut).start()
+
+    def at_distance(distance, act, cut):
+        if distance == 0:
+            act(cut, z)
+        else:
+            both_sides(distance, functools.partial(act, cut))
+
+    for cut in gather_parts:
+
+        @pl.when(has_up)
+        def _():
+            g_up(z, cut).start()
+
+        @pl.when(has_down)
+        def _():
+            g_down(z, cut).start()
+
+        spread_x(z, cut)
     for one in fetches:
         one.start()
     half_rows = all_rows // 2
@@ -211,7 +226,8 @@
     def core_arrived(half):
         for step in range(nz // 2):
             for px in range(2):
-                g_core(half * (nz // 2) + step, px, 1 - core).wait_recv()
+                for cut in gather_parts:
+                    g_core(half * (nz // 2) + step, px, 1 - core, cut).wait_recv()
 
     depth = 8 * LANES if blocks % 8 == 0 else LANES
 
@@ -219,7 +235,7 @@
         some = jnp.full((16, LANES), value.astype(jnp.float32)).astype(jnp.bfloat16)
         return jnp.concatenate([some] * (LANES // 16), axis=0)
 
-    def compute_hidden(half):
+    def compute_hidden(half, meanwhile=None):
         at_rows = half_at(half)
         sent = tok[at_rows, width:].astype(jnp.float32)
         lane = lax.broadcasted_iota(jnp.int32, sent.shape, 1)
@@ -242,6 +258,9 @@
         low = lax.fori_loop(
             0, width // depth, low_step, jnp.zeros((half_rows, LANES), jnp.float32)
         ).astype(jnp.bfloat16)
+
+        if meanwhile is not None:
+            meanwhile()
 
         def hidden_step(f, carry):
             left, right = [], []
@@ -300,21 +319,22 @@
         lax.fori_loop(0, blocks, output_step, 0, unroll=4)
 
     for distance in range(1, nz - 1):
-        both_sides(distance, pass_on)
-        if distance == 1:
-            cross(z)
-        else:
-            both_sides(distance - 1, cross)
+        for cut in gather_parts:
+            at_distance(distance, pass_on, cut)
+            at_distance(distance - 1, cross, cut)
     core_arrived(own_half)
     for one in fetches[:4]:
         one.wait()
+
     compute_hidden(own_half)
-    both_sides(nz - 1, pass_on)
-    both_sides(nz - 2, cross)
+    for cut in gather_parts:
+        at_distance(nz - 1, pass_on, cut)
+        at_distance(nz - 2, cross, cut)
     for one in fetches[4:]:
         one.wait()
     compute_part(own_half)
-    both_sides(nz - 1, cross)
+    for cut in gather_parts:
+        at_distance(nz - 1, cross, cut)
     core_arrived(other_half)
 
     def part_of(pz, px, pc):
@@ -329,116 +349,167 @@
             core_peer,
         )
 
-    def r_x(pz):
-        return remote(to_x.at[pz], from_x.at[pz], rx_send.at[pz], rx_recv.at[pz], x_peer)
-
-    def r_up(pz):
-        return remote(to_z.at[pz], from_low.at[pz], rz_send.at[pz], rlow_recv.at[pz], up_peer)
-
-    def r_down(pz):
-        return remote(to_z.at[pz], from_high.at[pz], rz_send.at[pz], rhigh_recv.at[pz], down_peer)
+    step_width = width // reduce_cuts
+    reduce_parts = range(reduce_cuts)
+
+    def columns_of(cut):
+        return pl.ds(cut * step_width, step_width)
+
+    def r_x(pz, cut):
+        at = columns_of(cut)
+        return remote(
+            to_x.at[pz, :, at],
+            from_x.at[pz, :, at],
+            rx_send.at[pz, cut],
+            rx_recv.at[pz, cut],
+            x_peer,
+        )
+
+    def r_up(pz, cut):
+        at = columns_of(cut)
+        return remote(
+            to_z.at[pz, :, at],
+            from_low.at[pz, :, at],
+            rz_send.at[pz, cut],
+            rlow_recv.at[pz, cut],
+            up_peer,
+        )
+
+    def r_down(pz, cut):
+        at = columns_of(cut)
+        return remote(
+            to_z.at[pz, :, at],
+            from_high.at[pz, :, at],
+            rz_send.at[pz, cut],
+            rhigh_recv.at[pz, cut],
+            down_peer,
+        )
 
     def wide(value):
         return value.astype(jnp.float32)
 
-    def ordered(act):
-        for distance in range(nz - 1, 0, -1):
-            both_sides(distance, act)
-
     def core_start(pz, px):
         r_core(pz, px).start()
 
     mate = own_half * nz + nz // 2 - 1 - z
-
-    def other_side(act):
-        near = jnp.where(own_half == 0, nz // 2, nz // 2 - 1)
-        toward = 1 - 2 * own_half
-        for step in range(nz // 2 - 1, -1, -1):
-            act(near + toward * step)
-
-    core_start(mate, 1 - x)
-    core_start(z, 1 - x)
-    core_start(mate, x)
-    core_start(z, x)
-    compute_hidden(other_half)
+    toward = 1 - 2 * own_half
+    near = jnp.where(own_half == 0, nz // 2, nz // 2 - 1)
+    far = near + toward * (nz // 2 - 1)
+    at_end = jnp.logical_or(z == 0, z == nz - 1)
+
+    def part_at(pz, px, cut):
+        at = pl.ds(pl.multiple_of(place(pz, px, core) * rows, rows), rows)
+        return wide(part[at, columns_of(cut)])
 
     def x_start(pz):
         r_core(pz, 1 - x).wait_recv()
-        total = wide(part_of(pz, 1 - x, core)[...]) + wide(from_core[pz, 1 - x])
-        to_x[pz] = total.astype(jnp.bfloat16)
-        r_x(pz).start()
-
-    x_start(mate)
-    x_start(z)
+        for cut in reduce_parts:
+            at = columns_of(cut)
+            total = part_at(pz, 1 - x, cut) + wide(from_core[pz, 1 - x, :, at])
+            to_x[pz, :, at] = total.astype(jnp.bfloat16)
+            r_x(pz, cut).start()
+
+    def local_sum(pz, cut):
+        r_x(pz, cut).wait_recv()
+        at = columns_of(cut)
+        total = part_at(pz, x, cut) + wide(from_core[pz, x, :, at])
+        return total + wide(from_x[pz, :, at])
+
+    def z_step(pz):
+        r_core(pz, x).wait_recv()
+        for cut in reduce_parts:
+            at = columns_of(cut)
+            acc[:, at] = local_sum(pz, cut)
+
+            @pl.when(pz < z)
+            def _():
+                @pl.when(has_up)
+                def _():
+                    r_down(pz, cut).wait_recv()
+                    acc[:, at] += wide(from_high[pz, :, at])
+
+                to_z[pz, :, at] = acc[:, at].astype(jnp.bfloat16)
+                r_down(pz, cut).start()
+
+            @pl.when(pz > z)
+            def _():
+                @pl.when(has_down)
+                def _():
+                    r_up(pz, cut).wait_recv()
+                    acc[:, at] += wide(from_low[pz, :, at])
+
+                to_z[pz, :, at] = acc[:, at].astype(jnp.bfloat16)
+                r_up(pz, cut).start()
+
+    for px in (1 - x, x):
+        core_start(mate, px)
+        core_start(z, px)
+
+    def near_sums():
+        x_start(mate)
+        x_start(z)
+
+    compute_hidden(other_half, near_sums)
     compute_part(other_half)
-    other_side(lambda pz: core_start(pz, 1 - x))
-    other_side(lambda pz: core_start(pz, x))
-    other_side(x_start)
-
-    def local_sum(pz):
-        r_core(pz, x).wait_recv()
-        r_x(pz).wait_recv()
-        total = wide(part_of(pz, x, core)[...]) + wide(from_core[pz, x])
-        return total + wide(from_x[pz])
-
-    def z_step(pz, lower):
-        acc[...] = local_sum(pz)
-        if lower:
-
-            @pl.when(has_up)
-            def _():
-                r_down(pz).wait_recv()
-                acc[...] += wide(from_high[pz])
-
-            to_z[pz] = acc[...].astype(jnp.bfloat16)
-            r_down(pz).start()
-        else:
-
-            @pl.when(has_down)
-            def _():
-                r_up(pz).wait_recv()
-                acc[...] += wide(from_low[pz])
-
-            to_z[pz] = acc[...].astype(jnp.bfloat16)
-            r_up(pz).start()
-
-    ordered(z_step)
-    acc[...] = local_sum(z)
-
-    @pl.when(has_up)
+    for px in (1 - x, x):
+        core_start(far, px)
+        core_start(near, px)
+
+    x_start(far)
+    x_start(near)
+
+    @pl.when(at_end)
     def _():
-        r_down(z).wait_recv()
-        acc[...] += wide(from_high[z])
-
-    @pl.when(has_down)
+        z_step(mate)
+
+    z_step(far)
+
+    @pl.when(jnp.logical_not(at_end))
     def _():
-        r_up(z).wait_recv()
-        acc[...] += wide(from_low[z])
-
-    out_ref[...] = acc[...].astype(jnp.bfloat16)
+        z_step(mate)
+
+    z_step(near)
+    r_core(z, x).wait_recv()
+    for cut in reduce_parts:
+        at = columns_of(cut)
+        acc[:, at] = local_sum(z, cut)
+
+        @pl.when(has_up)
+        def _():
+            r_down(z, cut).wait_recv()
+            acc[:, at] += wide(from_high[z, :, at])
+
+        @pl.when(has_down)
+        def _():
+            r_up(z, cut).wait_recv()
+            acc[:, at] += wide(from_low[z, :, at])
+
+        out_ref[:, at] = acc[:, at].astype(jnp.bfloat16)
 
     for pz in range(nz):
-        r_x(pz).wait_send()
         for px in range(2):
             r_core(pz, px).wait_send()
-
-        @pl.when(pz != z)
-        def _():
-            r_up(pz).wait_send()
+        for cut in reduce_parts:
+            r_x(pz, cut).wait_send()
+
+            @pl.when(pz != z)
+            def _():
+                r_up(pz, cut).wait_send()
 
     for pz in range(nz):
-
-        @pl.when(jnp.logical_and(has_up, pz <= z))
-        def _():
-            g_up(pz).wait_send()
-
-        @pl.when(jnp.logical_and(has_down, pz >= z))
-        def _():
-            g_down(pz).wait_send()
-
-        g_x(pz, x).wait_send()
-        for px in range(2):
-            g_core(pz, px, core).wait_send()
+        for cut in gather_parts:
+
+            @pl.when(jnp.logical_and(has_up, pz <= z))
+            def _():
+                g_up(pz, cut).wait_send()
+
+            @pl.when(jnp.logical_and(has_down, pz >= z))
+            def _():
+                g_down(pz, cut).wait_send()
+
+            g_x(pz, x, cut).wait_send()
+            for px in range(2):
+                g_core(pz, px, core, cut).wait_send()
 
 
 def tile_plan(base_index, keep, blocks):
@@ -513,8 +584,10 @@
         pl.BlockSpec(memory_space=space) for space in (pltpu.VMEM, pltpu.SMEM, pl.ANY)
     )
     dma = pltpu.SemaphoreType.DMA
+    gather_cuts = 2
+    reduce_cuts = 4 if blocks % 4 == 0 else 1
     return pl.pallas_call(
-        functools.partial(fused_kernel, nz),
+        functools.partial(fused_kernel, nz, gather_cuts, reduce_cuts),
         out_shape=jax.ShapeDtypeStruct((rows, width), bf16),
         in_specs=[vmem, vmem, smem] + [anywhere] * 7,
         out_specs=vmem,
@@ -540,20 +613,20 @@
             pltpu.VMEM((nz, rows, width), bf16),
             pltpu.VMEM((rows, width), f32),
             dma((7,)),
-            dma((nz,)),
-            dma((nz,)),
+            dma((nz, gather_cuts)),
+            dma((nz, gather_cuts)),
+            dma((nz, 2, gather_cuts)),
+            dma((nz, gather_cuts)),
+            dma((nz, gather_cuts)),
+            dma((nz, gather_cuts)),
+            dma((nz, 2, gather_cuts)),
             dma((nz, 2)),
-            dma((nz,)),
-            dma((nz,)),
-            dma((nz,)),
+            dma((nz, reduce_cuts)),
+            dma((nz, reduce_cuts)),
+            dma((nz, reduce_cuts)),
             dma((nz, 2)),
-            dma((nz, 2)),
-            dma((nz,)),
-            dma((nz,)),
-            dma((nz,)),
-            dma((nz, 2)),
-            dma((nz,)),
-            dma((nz,)),
+            dma((nz, reduce_cuts)),
+            dma((nz, reduce_cuts)),
         ],
         compiler_params=pltpu.CompilerParams(
             collective_id=0, has_side_effects=True, vmem_limit_bytes=60 << 20

time: 79.9 us -> 75.7 us (0.947)
  the two profiles are of different devices: /device:TPU:0 before, /device:TPU:16 now
where the time goes in v3:
time: 75.7 us; the launch traced here: 75.4 us
  Pallas kernels  68.3 us (90%)
  local copies, waits for them, and re-layouts  5.63 us (7%)
  other arithmetic  1.4 us (2%)
    pallas_call x1, Pallas kernels, per_device_fused(): pl.pallas_call(functools.partial(fused_kernel, nz, gather_cuts, reduce_cu...  68.3 us
    unnamed x5, local copies, waits for them, and re-layouts  4.67 us

profile of v3, /device:TPU:16, one launch (start us, length us, event | category | flops | bytes accessed | tf_op | source)
XLA Modules:
  0.0 75.4 jit_solution(2009460799219811352)
XLA Ops:
  0.0 0.8 %copy.27 = s32[16,8]{1,0:T(8,128)S(1)} copy(s32[16,8]{0,1:T(8,128)} %param.15) | data formatting | bytes 1024 | tf_op args[3]
  0.8 0.1 lt.32
  0.8 0.1 stack.31
  0.9 0.1 fusion.2
  1.1 0.1 convert_reduce_fusion.1
  1.2 0.1 convert_reduce_fusion
  1.3 0.8 %copy.28 = s32[1,16,8]{2,1,0:T(8,128)S(1)} copy(s32[1,16,8]{1,2,0:T(8,128)} %param.16) | data formatting | bytes 1024 | tf_op args[4]
  2.1 0.1 mul.11
  2.1 0.1 stack.32
  2.2 0.1 select_reduce_fusion
  2.4 0.1 slice_compare_fusion
  2.4 0.1 fusion.3
  2.5 0.6 stack.40.meta_ref
  3.1 0.8 %copy.25 = s32[16,8]{1,0:T(8,128)S(1)} copy(s32[16,8]{0,1:T(8,128)} %param.13) | data formatting | bytes 1024 | tf_op args[1]
  3.9 0.8 %copy.26 = f32[16,8]{1,0:T(8,128)S(1)} copy(f32[16,8]{0,1:T(8,128)} %param.14) | data formatting | bytes 1024 | tf_op args[2]
  4.7 0.1 select_reduce_fusion.3
  4.8 0.7 select_maximum_fusion.weight_ref
  5.4 68.3 %expert_layer.1 = bf16[16,7168]{1,0:T(8,128)(2,1)} custom-call(bf16[16,7168]{1,0:T(8,128)(2,1)} %tokens_ref.1, f32[16,128]{1,0:T(8,128)} %select_maximum_fusion.weight_ref, s32[8,128]{1,0:T(8,128)} %stack.40.meta_ref, bf16[128,128,128]{2,1,0:T(8,128)(2,1)} %bitcast.16, bf16[128,128,128]{2,1,0:T(8,128)(2,1)} %bitcast.17, bf16[128,128,128]{2,1,0:T(8,128)(2,1)} %bitcast.18, ...), custom_call_target="tpu_custom_call" | custom-call | tf_op jit(solution)/shard_map/expert_layer/pallas_call | solution.py:589
  73.8 1.6 %copy.32 = bf16[16,7168]{1,0:T(8,128)(2,1)} copy(bf16[16,7168]{1,0:T(8,128)(2,1)} %expert_layer.1) | data formatting | bytes 458752
  (3 shorter events, 0.0 us)

commit v4 on v3

--- a/solution.py
+++ b/solution.py
@@ -235,7 +235,7 @@
         some = jnp.full((16, LANES), value.astype(jnp.float32)).astype(jnp.bfloat16)
         return jnp.concatenate([some] * (LANES // 16), axis=0)
 
-    def compute_hidden(half, meanwhile=None):
+    def compute_hidden(half):
         at_rows = half_at(half)
         sent = tok[at_rows, width:].astype(jnp.float32)
         lane = lax.broadcasted_iota(jnp.int32, sent.shape, 1)
@@ -258,9 +258,6 @@
         low = lax.fori_loop(
             0, width // depth, low_step, jnp.zeros((half_rows, LANES), jnp.float32)
         ).astype(jnp.bfloat16)
-
-        if meanwhile is not None:
-            meanwhile()
 
         def hidden_step(f, carry):
             left, right = [], []
@@ -333,9 +330,6 @@
     for one in fetches[4:]:
         one.wait()
     compute_part(own_half)
-    for cut in gather_parts:
-        at_distance(nz - 1, cross, cut)
-    core_arrived(other_half)
 
     def part_of(pz, px, pc):
         return part.at[pl.ds(pl.multiple_of(place(pz, px, pc) * rows, rows), rows)]
@@ -444,12 +438,12 @@
     for px in (1 - x, x):
         core_start(mate, px)
         core_start(z, px)
-
-    def near_sums():
-        x_start(mate)
-        x_start(z)
-
-    compute_hidden(other_half, near_sums)
+    for cut in gather_parts:
+        at_distance(nz - 1, cross, cut)
+    x_start(mate)
+    x_start(z)
+    core_arrived(other_half)
+    compute_hidden(other_half)
     compute_part(other_half)
     for px in (1 - x, x):
         core_start(far, px)

time: 75.7 us -> 76.7 us (1.013)
  Pallas kernels: 68.3 us -> 69.2 us
    pallas_call x1, Pallas kernels: 68.3 us -> 69.2 us  [per_device_fused(): pl.pallas_call(functools.partial(fused_kernel, nz, gather_cuts, reduce_cu...]
where the time goes in v4:
time: 76.7 us; the launch traced here: 76.3 us
  Pallas kernels  69.2 us (90%)
  local copies, waits for them, and re-layouts  5.63 us (7%)
  other arithmetic  1.4 us (2%)
    pallas_call x1, Pallas kernels, per_device_fused(): pl.pallas_call(functools.partial(fused_kernel, nz, gather_cuts, reduce_cu...  69.2 us
    unnamed x5, local copies, waits for them, and re-layouts  4.67 us

profile of v4, /device:TPU:16, one launch (start us, length us, event | category | flops | bytes accessed | tf_op | source)
XLA Modules:
  0.0 76.3 jit_solution(11353793048820486047)
XLA Ops:
  0.0 0.8 copy.27
  0.8 0.1 lt.32
  0.8 0.1 stack.31
  0.9 0.1 fusion.2
  1.1 0.1 convert_reduce_fusion.1
  1.2 0.1 convert_reduce_fusion
  1.3 0.8 copy.28
  2.1 0.1 mul.11
  2.1 0.1 stack.32
  2.2 0.1 select_reduce_fusion
  2.4 0.1 slice_compare_fusion
  2.4 0.1 fusion.3
  2.5 0.6 stack.40.meta_ref
  3.1 0.8 copy.25
  3.9 0.8 copy.26
  4.7 0.1 select_reduce_fusion.3
  4.8 0.7 select_maximum_fusion.weight_ref
  5.4 69.2 %expert_layer.1 = bf16[16,7168]{1,0:T(8,128)(2,1)} custom-call(bf16[16,7168]{1,0:T(8,128)(2,1)} %tokens_ref.1, f32[16,128]{1,0:T(8,128)} %select_maximum_fusion.weight_ref, s32[8,128]{1,0:T(8,128)} %stack.40.meta_ref, bf16[128,128,128]{2,1,0:T(8,128)(2,1)} %bitcast.16, bf16[128,128,128]{2,1,0:T(8,128)(2,1)} %bitcast.17, bf16[128,128,128]{2,1,0:T(8,128)(2,1)} %bitcast.18, ...), custom_call_target="tpu_custom_call" | custom-call | tf_op jit(solution)/shard_map/expert_layer/pallas_call | solution.py:583
  74.6 1.6 %copy.32 = bf16[16,7168]{1,0:T(8,128)(2,1)} copy(bf16[16,7168]{1,0:T(8,128)(2,1)} %expert_layer.1) | data formatting | bytes 458752
  (3 shorter events, 0.0 us)

commit v5 on v3

--- a/solution.py
+++ b/solution.py
@@ -15,7 +15,10 @@
     gather_cuts,
     reduce_cuts,
     tokens_ref,
-    weight_ref,
+    routes_ref,
+    choice_ref,
+    index_ref,
+    keep_ref,
     meta_ref,
     gate_hbm,
     up_hbm,
@@ -115,13 +118,18 @@
 
     own_rows = pl.ds(pl.multiple_of(me * rows, rows), rows)
     tok[own_rows, :width] = tokens_ref[...]
-    weights = weight_ref[...]
-    lane = lax.broadcasted_iota(jnp.int32, weights.shape, 1)
+    experts = 4 * nz
+    lane = lax.broadcasted_iota(jnp.int32, (rows, LANES), 1)
+    expert = lax.rem(lane, experts)
+    weights = jnp.zeros((rows, LANES), jnp.float32)
+    for k in range(routes_ref.shape[1]):
+        named = routes_ref[:, k : k + 1] == expert
+        weights = weights + jnp.where(named, choice_ref[:, k : k + 1], 0.0)
+    weights = jnp.where(lane < 3 * experts, weights, 0.0)
     high = weights.astype(jnp.bfloat16)
     rest = weights - high.astype(jnp.float32)
     middle = rest.astype(jnp.bfloat16)
     low_part = rest - middle.astype(jnp.float32)
-    experts = 4 * nz
     tok[own_rows, width:] = jnp.where(
         lane < experts,
         high.astype(jnp.float32),
@@ -235,7 +243,7 @@
         some = jnp.full((16, LANES), value.astype(jnp.float32)).astype(jnp.bfloat16)
         return jnp.concatenate([some] * (LANES // 16), axis=0)
 
-    def compute_hidden(half, meanwhile=None):
+    def compute_hidden(half, meanwhile=None, midway=None):
         at_rows = half_at(half)
         sent = tok[at_rows, width:].astype(jnp.float32)
         lane = lax.broadcasted_iota(jnp.int32, sent.shape, 1)
@@ -266,8 +274,8 @@
             left, right = [], []
             for k in range(per_block):
                 pair = f * per_block + k
-                left.append(columns[meta_ref[0, pair]])
-                keep = keep_tile(meta_ref[1, pair])
+                left.append(columns[index_ref[f, k]])
+                keep = keep_tile(keep_ref[f, k])
                 right.append(jnp.concatenate([gate_v[pair] * keep, up_v[pair] * keep], axis=1))
             units = pl.ds(pl.multiple_of(f * LANES, LANES), LANES)
             left.append(low)
@@ -281,9 +289,14 @@
             hidden[f] = (gate / (1.0 + jnp.exp(-gate)) * up).astype(jnp.bfloat16)
             return carry
 
-        lax.fori_loop(0, count_blocks, hidden_step, 0, unroll=2)
-
-    def compute_part(half):
+        if midway is None:
+            lax.fori_loop(0, count_blocks, hidden_step, 0, unroll=2)
+        else:
+            lax.fori_loop(0, count_blocks // 2, hidden_step, 0, unroll=2)
+            midway()
+            lax.fori_loop(count_blocks // 2, count_blocks, hidden_step, 0, unroll=2)
+
+    def compute_part(half, midway=None):
         at_rows = half_at(half)
 
         def squeeze_step(f, total):
@@ -295,11 +308,12 @@
         ).astype(jnp.bfloat16)
 
         def down_step(step, total):
-            pair = meta_ref[2, step]
-            tile = down_v[pair] * keep_tile(meta_ref[4, step])
-            again = meta_ref[5, step].astype(jnp.float32)
+            pair = meta_ref[0, step]
+            f = meta_ref[1, step]
+            tile = down_v[pair] * keep_tile(keep_ref[f, pair - f * per_block])
+            again = meta_ref[2, step].astype(jnp.float32)
             total = total * again + jnp.dot(
-                hidden[meta_ref[3, step]], tile, preferred_element_type=jnp.float32
+                hidden[f], tile, preferred_element_type=jnp.float32
             )
             segment[step] = total
             return total
@@ -308,10 +322,13 @@
             0, pairs, down_step, jnp.zeros((half_rows, LANES), jnp.float32), unroll=8
         )
 
+        if midway is not None:
+            midway()
+
         def output_step(d, carry):
             at = pl.ds(pl.multiple_of(d * LANES, LANES), LANES)
             value = jnp.dot(squeezed, last_v[:, at], preferred_element_type=jnp.float32)
-            value = value + segment[meta_ref[6, d]] * meta_ref[7, d].astype(jnp.float32)
+            value = value + segment[meta_ref[3, d]] * meta_ref[4, d].astype(jnp.float32)
             value = value.astype(jnp.bfloat16).astype(jnp.float32) * scale[...]
             part[at_rows, at] = value.astype(jnp.bfloat16)
             return carry
@@ -326,16 +343,20 @@
     for one in fetches[:4]:
         one.wait()
 
-    compute_hidden(own_half)
-    for cut in gather_parts:
+
+    def forward(cut):
         at_distance(nz - 1, pass_on, cut)
         at_distance(nz - 2, cross, cut)
+
+    def forward_early():
+        for cut in range(gather_cuts - 1):
+            forward(cut)
+
+    compute_hidden(own_half, None, forward_early)
+    forward(gather_cuts - 1)
     for one in fetches[4:]:
         one.wait()
-    compute_part(own_half)
-    for cut in gather_parts:
-        at_distance(nz - 1, cross, cut)
-    core_arrived(other_half)
+    compute_part(own_half, lambda: at_distance(nz - 1, cross, 0))
 
     def part_of(pz, px, pc):
         return part.at[pl.ds(pl.multiple_of(place(pz, px, pc) * rows, rows), rows)]
@@ -449,6 +470,9 @@
         x_start(mate)
         x_start(z)
 
+    for cut in range(1, gather_cuts):
+        at_distance(nz - 1, cross, cut)
+    core_arrived(other_half)
     compute_hidden(other_half, near_sums)
     compute_part(other_half)
     for px in (1 - x, x):
@@ -512,7 +536,7 @@
                 g_core(pz, px, core, cut).wait_send()
 
 
-def tile_plan(base_index, keep, blocks):
+def tile_plan(base_index, blocks):
     flat = base_index.reshape(-1)
     pairs = flat.shape[0]
     place = jnp.arange(pairs, dtype=jnp.int32)
@@ -521,9 +545,7 @@
     )
     rank = jnp.sum(ahead.astype(jnp.int32), axis=0)
     chosen = (rank[:, None] == place[None, :]).astype(jnp.int32)
-    keep = keep.reshape(-1)
     order = jnp.sum(chosen * place[:, None], axis=0)
-    sorted_keep = jnp.sum(chosen * keep[:, None], axis=0)
     sorted_block = jnp.sum(chosen * flat[:, None], axis=0)
     again = jnp.concatenate(
         [jnp.zeros((1,), jnp.int32), (sorted_block[1:] == sorted_block[:-1]).astype(jnp.int32)]
@@ -538,11 +560,8 @@
 
     return jnp.stack(
         [
-            row(flat),
-            row(keep),
             row(order),
             row(order // base_index.shape[1]),
-            row(sorted_keep),
             row(again),
             row(jnp.maximum(upto - 1, 0)),
             row(used),
@@ -571,12 +590,7 @@
     count_blocks, per_block = base_index.shape
     pairs = count_blocks * per_block
     all_rows = rows * experts
-    named = routes[:, :, None] == jnp.arange(experts, dtype=jnp.int32)[None, None, :]
-    weights = jnp.sum(jnp.where(named, route_weight[:, :, None], 0.0), axis=1)
-    weights = jnp.pad(
-        jnp.concatenate([weights] * 3, axis=1), ((0, 0), (0, LANES - 3 * experts))
-    )
-    meta = tile_plan(base_index, expert_mask[0], blocks)
+    meta = tile_plan(base_index, blocks)
     lift = delta_gate_up[0]
     units = lift.shape[2]
     bf16, f32 = jnp.bfloat16, jnp.float32
@@ -589,7 +603,7 @@
     return pl.pallas_call(
         functools.partial(fused_kernel, nz, gather_cuts, reduce_cuts),
         out_shape=jax.ShapeDtypeStruct((rows, width), bf16),
-        in_specs=[vmem, vmem, smem] + [anywhere] * 7,
+        in_specs=[vmem, vmem, vmem, smem, smem, smem] + [anywhere] * 7,
         out_specs=vmem,
         scratch_shapes=[
             pltpu.VMEM((all_rows, width + LANES), bf16),
@@ -634,7 +648,10 @@
         name="expert_layer",
     )(
         tokens,
-        weights,
+        routes,
+        route_weight,
+        base_index,
+        expert_mask[0],
         meta,
         base_gate.reshape(pairs, LANES, LANES),
         base_up.reshape(pairs, LANES, LANES),

time: 75.7 us -> 77.7 us (1.026)
  local copies, waits for them, and re-layouts: 5.63 us -> 7.16 us
  Pallas kernels: 68.3 us -> 69.3 us
  other arithmetic: 1.4 us -> 0.61 us
    squeeze x0 -> x1, local copies, waits for them, and re-layouts: none -> 1.35 us  [per_device_fused(): expert_mask[0]]
    pallas_call x1, Pallas kernels: 68.3 us -> 69.3 us  [per_device_fused(): pl.pallas_call(functools.partial(fused_kernel, nz, gather_cuts, reduce_cu...]
    unnamed x5 -> x6, local copies, waits for them, and re-layouts: 4.67 us -> 5.11 us
where the time goes in v5:
time: 77.7 us; the launch traced here: 77.2 us
  Pallas kernels  69.3 us (89%)
  local copies, waits for them, and re-layouts  7.16 us (9%)
    pallas_call x1, Pallas kernels, per_device_fused(): pl.pallas_call(functools.partial(fused_kernel, nz, gather_cuts, reduce_cu...  69.3 us
    unnamed x6, local copies, waits for them, and re-layouts  5.11 us

profile of v5, /device:TPU:16, one launch (start us, length us, event | category | flops | bytes accessed | tf_op | source)
XLA Modules:
  0.0 77.2 jit_solution(9027895258084297356)
XLA Ops:
  0.0 0.8 copy.26.index_ref
  0.8 0.0 copy-start
  0.8 0.1 lt.32
  0.8 0.1 fusion.2
  1.0 0.1 convert_reduce_fusion.1
  1.1 0.1 convert_reduce_fusion
  1.2 0.1 select_reduce_fusion
  1.3 0.1 slice_compare_fusion
  1.4 0.1 fusion.3
  1.5 0.6 stack.28.meta_ref
  2.1 1.4 %copy.24.routes_ref = s32[16,8]{1,0:T(8,128)} copy(s32[16,8]{0,1:T(8,128)} %param.13) | data formatting | bytes 1024 | tf_op args[1]
  3.5 1.4 %copy.25.choice_ref = f32[16,8]{1,0:T(8,128)} copy(f32[16,8]{0,1:T(8,128)} %param.14) | data formatting | bytes 1024 | tf_op args[2]
  4.8 1.3 %copy.27.keep_ref = s32[16,8]{1,0:T(8,128)} copy(s32[16,8]{0,1:T(8,128)} %bitcast.23) | data formatting | bytes 1024 | tf_op jit(solution)/shard_map/squeeze | solution.py:654
  6.2 0.0 copy-done
  6.2 69.3 %expert_layer.1 = bf16[16,7168]{1,0:T(8,128)(2,1)} custom-call(bf16[16,7168]{1,0:T(8,128)(2,1)} %tokens_ref.1, s32[16,8]{1,0:T(8,128)} %copy.24.routes_ref, f32[16,8]{1,0:T(8,128)} %copy.25.choice_ref, s32[16,8]{1,0:T(8,128)} %copy-done, s32[16,8]{1,0:T(8,128)} %copy.27.keep_ref, s32[5,128]{1,0:T(8,128)} %stack.28.meta_ref, bf16[128,128,128]{2,1,0:T(8,128)(2,1)} %bitcast.16, ...), custom_call_target="tpu_custom_call" | custom-call | tf_op jit(solution)/shard_map/expert_layer/pallas_call | solution.py:603
  75.5 1.6 %copy.29 = bf16[16,7168]{1,0:T(8,128)(2,1)} copy(bf16[16,7168]{1,0:T(8,128)(2,1)} %expert_layer.1) | data formatting | bytes 458752
  (3 shorter events, 0.0 us)
Async XLA Ops:
  0.8 5.4 %copy-start = (s32[16,8]{1,0:T(8,128)}, s32[16,8]{1,0:T(8,128)S(1)}, u32[]{:S(2)}) copy-start(s32[16,8]{1,0:T(8,128)S(1)} %copy.26.index_ref) | copy-start | bytes 1540

commit v6 on v3

--- a/solution.py
+++ b/solution.py
@@ -16,6 +16,8 @@
     reduce_cuts,
     tokens_ref,
     weight_ref,
+    index_ref,
+    keep_ref,
     meta_ref,
     gate_hbm,
     up_hbm,
@@ -266,8 +268,8 @@
             left, right = [], []
             for k in range(per_block):
                 pair = f * per_block + k
-                left.append(columns[meta_ref[0, pair]])
-                keep = keep_tile(meta_ref[1, pair])
+                left.append(columns[index_ref[k, f]])
+                keep = keep_tile(keep_ref[k, f])
                 right.append(jnp.concatenate([gate_v[pair] * keep, up_v[pair] * keep], axis=1))
             units = pl.ds(pl.multiple_of(f * LANES, LANES), LANES)
             left.append(low)
@@ -295,11 +297,12 @@
         ).astype(jnp.bfloat16)
 
         def down_step(step, total):
-            pair = meta_ref[2, step]
-            tile = down_v[pair] * keep_tile(meta_ref[4, step])
-            again = meta_ref[5, step].astype(jnp.float32)
+            pair = meta_ref[0, step]
+            f = meta_ref[1, step]
+            tile = down_v[pair] * keep_tile(keep_ref[pair - f * per_block, f])
+            again = meta_ref[2, step].astype(jnp.float32)
             total = total * again + jnp.dot(
-                hidden[meta_ref[3, step]], tile, preferred_element_type=jnp.float32
+                hidden[f], tile, preferred_element_type=jnp.float32
             )
             segment[step] = total
             return total
@@ -311,7 +314,7 @@
         def output_step(d, carry):
             at = pl.ds(pl.multiple_of(d * LANES, LANES), LANES)
             value = jnp.dot(squeezed, last_v[:, at], preferred_element_type=jnp.float32)
-            value = value + segment[meta_ref[6, d]] * meta_ref[7, d].astype(jnp.float32)
+            value = value + segment[meta_ref[3, d]] * meta_ref[4, d].astype(jnp.float32)
             value = value.astype(jnp.bfloat16).astype(jnp.float32) * scale[...]
             part[at_rows, at] = value.astype(jnp.bfloat16)
             return carry
@@ -512,8 +515,9 @@
                 g_core(pz, px, core, cut).wait_send()
 
 
-def tile_plan(base_index, keep, blocks):
-    flat = base_index.reshape(-1)
+def tile_plan(index_rows, blocks):
+    per_block, count_blocks = index_rows.shape
+    flat = index_rows.reshape(-1)
     pairs = flat.shape[0]
     place = jnp.arange(pairs, dtype=jnp.int32)
     ahead = (flat[:, None] < flat[None, :]) | (
@@ -521,9 +525,10 @@
     )
     rank = jnp.sum(ahead.astype(jnp.int32), axis=0)
     chosen = (rank[:, None] == place[None, :]).astype(jnp.int32)
-    keep = keep.reshape(-1)
-    order = jnp.sum(chosen * place[:, None], axis=0)
-    sorted_keep = jnp.sum(chosen * keep[:, None], axis=0)
+    unit_block = place % count_blocks
+    stored = unit_block * per_block + place // count_blocks
+    order = jnp.sum(chosen * stored[:, None], axis=0)
+    order_block = jnp.sum(chosen * unit_block[:, None], axis=0)
     sorted_block = jnp.sum(chosen * flat[:, None], axis=0)
     again = jnp.concatenate(
         [jnp.zeros((1,), jnp.int32), (sorted_block[1:] == sorted_block[:-1]).astype(jnp.int32)]
@@ -538,11 +543,8 @@
 
     return jnp.stack(
         [
-            row(flat),
-            row(keep),
             row(order),
-            row(order // base_index.shape[1]),
-            row(sorted_keep),
+            row(order_block),
             row(again),
             row(jnp.maximum(upto - 1, 0)),
             row(used),
@@ -571,12 +573,13 @@
     count_blocks, per_block = base_index.shape
     pairs = count_blocks * per_block
     all_rows = rows * experts
-    named = routes[:, :, None] == jnp.arange(experts, dtype=jnp.int32)[None, None, :]
-    weights = jnp.sum(jnp.where(named, route_weight[:, :, None], 0.0), axis=1)
+    named = routes.T[:, None, :] == jnp.arange(experts, dtype=jnp.int32)[None, :, None]
+    weights = jnp.sum(jnp.where(named, route_weight.T[:, None, :], 0.0), axis=0)
     weights = jnp.pad(
-        jnp.concatenate([weights] * 3, axis=1), ((0, 0), (0, LANES - 3 * experts))
-    )
-    meta = tile_plan(base_index, expert_mask[0], blocks)
+        jnp.concatenate([weights] * 3, axis=0), ((0, LANES - 3 * experts), (0, 0))
+    ).T
+    index_rows = base_index.T
+    meta = tile_plan(index_rows, blocks)
     lift = delta_gate_up[0]
     units = lift.shape[2]
     bf16, f32 = jnp.bfloat16, jnp.float32
@@ -589,7 +592,7 @@
     return pl.pallas_call(
         functools.partial(fused_kernel, nz, gather_cuts, reduce_cuts),
         out_shape=jax.ShapeDtypeStruct((rows, width), bf16),
-        in_specs=[vmem, vmem, smem] + [anywhere] * 7,
+        in_specs=[vmem, vmem, smem, smem, smem] + [anywhere] * 7,
         out_specs=vmem,
         scratch_shapes=[
             pltpu.VMEM((all_rows, width + LANES), bf16),
@@ -635,6 +638,8 @@
     )(
         tokens,
         weights,
+        index_rows,
+        expert_mask[0].T,
         meta,
         base_gate.reshape(pairs, LANES, LANES),
         base_up.reshape(pairs, LANES, LANES),

time: 75.7 us -> 74 us (0.978)
  local copies, waits for them, and re-layouts: 5.63 us -> 3.09 us
    unnamed x5 -> x1, local copies, waits for them, and re-layouts: 4.67 us -> 1.64 us
where the time goes in v6:
time: 74 us; the launch traced here: 73.7 us
  Pallas kernels  68.5 us (93%)
  local copies, waits for them, and re-layouts  3.09 us (4%)
  other arithmetic  2.03 us (3%)
    pallas_call x1, Pallas kernels, per_device_fused(): pl.pallas_call(functools.partial(fused_kernel, nz, gather_cuts, reduce_cu...  68.5 us
    unnamed x1, local copies, waits for them, and re-layouts  1.64 us

profile of v6, /device:TPU:16, one launch (start us, length us, event | category | flops | bytes accessed | tf_op | source)
XLA Modules:
  0.0 73.7 jit_solution(6811491587489912939)
XLA Ops:
  0.0 0.8 %lt.38 = s32[128]{0:T(128)S(1)} reshape(s32[8,16]{1,0:T(8,128)} %bitcast.30) | data formatting | bytes 1024 | tf_op jit(solution)/shard_map/lt | solution.py:523
  0.8 0.1 fusion.2
  0.9 0.1 convert_reduce_fusion.1
  1.0 0.1 convert_reduce_fusion
  1.1 0.1 select_reduce_fusion
  1.3 0.1 slice_compare_fusion
  1.4 0.1 fusion.6
  1.4 0.6 stack.31.meta_ref
  2.1 0.7 select_reduce_fusion.3
  2.8 0.1 copy.13
  2.8 0.7 fusion.3.weight_ref
  3.5 68.5 %expert_layer.1 = bf16[16,7168]{1,0:T(8,128)(2,1)} custom-call(bf16[16,7168]{1,0:T(8,128)(2,1)} %tokens_ref.1, f32[16,128]{1,0:T(8,128)} %fusion.3.weight_ref, s32[8,16]{1,0:T(8,128)} %bitcast.31, s32[8,16]{1,0:T(8,128)} %bitcast.32, s32[5,128]{1,0:T(8,128)} %stack.31.meta_ref, bf16[128,128,128]{2,1,0:T(8,128)(2,1)} %bitcast.23, ...), custom_call_target="tpu_custom_call" | custom-call | tf_op jit(solution)/shard_map/expert_layer/pallas_call | solution.py:592
  72.0 1.6 %copy.17 = bf16[16,7168]{1,0:T(8,128)(2,1)} copy(bf16[16,7168]{1,0:T(8,128)(2,1)} %expert_layer.1) | data formatting | bytes 458752
  (4 shorter events, 0.0 us)

commit v7 on v6

--- a/solution.py
+++ b/solution.py
@@ -283,7 +283,7 @@
             hidden[f] = (gate / (1.0 + jnp.exp(-gate)) * up).astype(jnp.bfloat16)
             return carry
 
-        lax.fori_loop(0, count_blocks, hidden_step, 0, unroll=2)
+        lax.fori_loop(0, count_blocks, hidden_step, 0, unroll=4)
 
     def compute_part(half):
         at_rows = half_at(half)
@@ -308,7 +308,7 @@
             return total
 
         lax.fori_loop(
-            0, pairs, down_step, jnp.zeros((half_rows, LANES), jnp.float32), unroll=8
+            0, pairs, down_step, jnp.zeros((half_rows, LANES), jnp.float32), unroll=16
         )
 
         def output_step(d, carry):
@@ -319,7 +319,7 @@
             part[at_rows, at] = value.astype(jnp.bfloat16)
             return carry
 
-        lax.fori_loop(0, blocks, output_step, 0, unroll=4)
+        lax.fori_loop(0, blocks, output_step, 0, unroll=8)
 
     for distance in range(1, nz - 1):
         for cut in gather_parts:

time: 74 us -> 68.8 us (0.930)
  Pallas kernels: 68.5 us -> 62.9 us
    pallas_call x1, Pallas kernels: 68.5 us -> 62.9 us  [per_device_fused(): pl.pallas_call(functools.partial(fused_kernel, nz, gather_cuts, reduce_cu...]
where the time goes in v7:
time: 68.8 us; the launch traced here: 68 us
  Pallas kernels  62.9 us (91%)
  local copies, waits for them, and re-layouts  3.09 us (4%)
  other arithmetic  2.03 us (3%)
    pallas_call x1, Pallas kernels, per_device_fused(): pl.pallas_call(functools.partial(fused_kernel, nz, gather_cuts, reduce_cu...  62.9 us
    unnamed x1, local copies, waits for them, and re-layouts  1.64 us

profile of v7, /device:TPU:16, one launch (start us, length us, event | category | flops | bytes accessed | tf_op | source)
XLA Modules:
  0.0 68.0 jit_solution(14703037216897593310)
XLA Ops:
  0.0 0.8 %lt.38 = s32[128]{0:T(128)S(1)} reshape(s32[8,16]{1,0:T(8,128)} %bitcast.30) | data formatting | bytes 1024 | tf_op jit(solution)/shard_map/lt | solution.py:523
  0.8 0.1 fusion.2
  0.9 0.1 convert_reduce_fusion.1
  1.0 0.1 convert_reduce_fusion
  1.1 0.1 select_reduce_fusion
  1.3 0.1 slice_compare_fusion
  1.4 0.1 fusion.6
  1.4 0.6 stack.31.meta_ref
  2.1 0.7 %select_reduce_fusion.3 = f32[16,16]{1,0:T(8,128)S(1)} fusion(f32[8,16]{1,0:T(8,128)} %bitcast.33, s32[8,16]{1,0:T(8,128)} %bitcast.34), kind=kLoop, calls=%fused_computation.6 | loop fusion | flops 5888 | bytes 2048 | tf_op jit(solution)/shard_map/reduce_sum | solution.py:577
  2.8 0.1 copy.13
  2.8 0.7 fusion.3.weight_ref
  3.5 62.9 %expert_layer.1 = bf16[16,7168]{1,0:T(8,128)(2,1)} custom-call(bf16[16,7168]{1,0:T(8,128)(2,1)} %tokens_ref.1, f32[16,128]{1,0:T(8,128)} %fusion.3.weight_ref, s32[8,16]{1,0:T(8,128)} %bitcast.31, s32[8,16]{1,0:T(8,128)} %bitcast.32, s32[5,128]{1,0:T(8,128)} %stack.31.meta_ref, bf16[128,128,128]{2,1,0:T(8,128)(2,1)} %bitcast.23, ...), custom_call_target="tpu_custom_call" | custom-call | tf_op jit(solution)/shard_map/expert_layer/pallas_call | solution.py:592
  66.4 1.6 %copy.17 = bf16[16,7168]{1,0:T(8,128)(2,1)} copy(bf16[16,7168]{1,0:T(8,128)(2,1)} %expert_layer.1) | data formatting | bytes 458752
  (4 shorter events, 0.0 us)
